TPU v7x, 256 devices: a whole 4x4x8 slice. The times are simulated.
256 devices in a mesh: batch: 64 (over z, x, core), row: 2 (over y_lo), col: 2 (over y_hi).
Axes of the slice: x: 4, y: 4 (y_hi: 2, y_lo: 2; y = y_hi * 2 + y_lo), z: 8, core: 2. Of those that a mesh axis runs over, the one named last changes fastest.
Arguments:
- basis_values: bfloat16 [256, 192, 2048], P(('batch', 'row', 'col')), may hold values from -6 to 6
- density_matrix: bfloat16 [256, 3, 192, 192], P(('batch', 'row', 'col')), may hold values from -0.03125 to 0.03125
- points: float32 [256, 3, 2048], P(('batch', 'row', 'col')), may hold values from -2 to 2
- weights: float32 [256, 2048], P(('batch', 'row', 'col')), may hold values from 0.128 to 1.28
- intersection: int32 [256, 32], P(('batch', 'row', 'col')), may hold values from 0 to 255, as said below
- basis_index: int32 [256, 192], P(('batch', 'row', 'col')), may hold values from 0 to 1535, as said below
- atom_positions: float32 [3, 256], replicated, may hold values from -2 to 2
- shell_blocks: int32 [256], replicated, may hold values from 1 to 8
- shell_widths: float32 [64], replicated, may hold values from 0.03125 to 0.0625
- green: bfloat16 [256, 8, 4096], P('batch'), may hold values from -0.0009765625 to 0.0009765625
Outputs:
- potential: bfloat16 [256, 12288], P('batch')
- hamiltonian: bfloat16 [3, 1536, 1536], P(None, 'row', 'col')
Inputs may be any that keep to these rules, and one draw needn't show every extreme that they name: `intersection`: within a batch the 32 atom numbers are distinct. The owner of atom a is a // 4; no owner holds more than 1 of one batch's atoms, and among the batches with equal row and col index one owner holds exactly 1 of the atoms of every such batch. `basis_index`: within a batch the numbers are distinct, and its q-th run of 96 entries lies in [q * 768, (q + 1) * 768).
All inputs are finite; a program needn't handle non-finite values.
Results may differ from a plain program's by a relative error of at most 0.0095.
Values may be sent and summed in bfloat16 or wider, within the bound.
A program may use at most 128 MiB of HBM per device.

v0:
```python
import jax
import jax.numpy as jnp
from jax import lax
from jax.sharding import Mesh
from jax.sharding import PartitionSpec as P

S = 64
DEG = 8
NB = 1536
BATCH = ("batch_0", "batch_1", "batch_2")
BATCH_ROW_COL = ("batch_0", "batch_1", "batch_2", "row", "col")


def from_everyone(x, axis):
    count = lax.axis_size(axis)
    return lax.all_to_all(jnp.broadcast_to(x[None], (count, *x.shape)), axis, 0, 0, tiled=True)


def of_everyone(x, axis):
    everything = from_everyone(x, axis)
    return jnp.sum(everything, axis=0)


def split_up(x, dim, count):
    lengths = x.shape
    parts = x.reshape(*lengths[:dim], count, lengths[dim] // count, *lengths[dim + 1 :])
    return jnp.moveaxis(parts, dim, 0)


def in_order(parts, dim):
    lengths = list(parts.shape[1:])
    lengths[dim] *= parts.shape[0]
    return jnp.moveaxis(parts, 0, dim).reshape(lengths)


def joined_exchange(x, axis, axes, splits, concats):
    sizes = [lax.axis_size(a) for a in axes]
    parts = split_up(x, splits[0], sizes[0])
    parts = jnp.moveaxis(split_up(parts, splits[1] + 1, sizes[1]), 0, 1)
    inside = parts.shape[2:]
    parts = parts.reshape(-1, *inside)
    parts = lax.all_to_all(parts, axis, split_axis=0, concat_axis=0, tiled=True)
    parts = in_order(parts.reshape(*sizes, *inside), concats[0] + 1)
    return in_order(parts, concats[1])


def scatter_axes(x, axes, dim):
    if not axes:
        return x
    nearer = lax.psum_scatter(x, axes[0], scatter_dimension=dim, tiled=True)
    return scatter_axes(nearer, axes[1:], dim)


def gather_in_order(x, axes, turns):
    parts = x[None]
    for k in turns:
        parts = lax.all_gather(parts, axes[k], axis=0, tiled=True)
    carried = [lax.axis_size(axes[k]) for k in reversed(turns)]
    parts = parts.reshape(*carried, *x.shape)
    turned = sorted(range(len(turns)), key=lambda place: turns[len(turns) - 1 - place])
    return parts.transpose(*turned, *range(len(turns), parts.ndim)).reshape(-1, *x.shape)


def gathered_by_axis(x, axes, turns, dim):
    return in_order(gather_in_order(x, axes, turns), dim)


def chebyshev(values, count):
    terms = [jnp.ones_like(values), values]
    for order in range(2, count):
        terms.append(2.0 * values * terms[-1] - terms[-2])
    return jnp.stack(terms[:count], axis=0)


def atom_tables(spots, centre, blocks, shell_widths):
    delta = spots - centre[:, None]
    dist = jnp.sqrt(jnp.sum(delta * delta, axis=0) + 0.01)
    unit = delta / dist[None, :]
    shells = shell_widths.shape[0]
    middle = 4.0 * jnp.arange(shells).astype(jnp.float32) / shells
    live = jnp.arange(shells) < 8 * blocks
    bump = jnp.exp(-jnp.square((dist[None, :] - middle[:, None]) / shell_widths[:, None]))
    radial = jnp.where(live[:, None], bump, jnp.zeros_like(bump))
    polar = chebyshev(unit[2], DEG)
    side = chebyshev(unit[0], DEG)
    angular = (polar[:, None, :] * side[None, :, :]).reshape(DEG * DEG, spots.shape[1])
    return (radial, angular.astype(jnp.bfloat16))


def apply_green(charges, kernels):
    shaped = charges.astype(jnp.bfloat16).reshape(-1, 3, S, DEG, DEG)
    kernel_rows = kernels.reshape(-1, DEG, S, S)
    result = jnp.einsum(
        "xast,xctam->xcsam", kernel_rows, shaped, preferred_element_type=jnp.float32
    )
    return result.astype(jnp.bfloat16).reshape(-1, 3 * S * DEG * DEG)


def on_device(
    basis_values,
    density_matrix,
    points,
    weights,
    intersection,
    basis_index,
    atom_positions,
    shell_blocks,
    shell_widths,
    green,
):
    phi = basis_values[0]
    dens = density_matrix[0]
    spots = points[0]
    measure = weights[0]
    atoms = intersection[0]
    labels = basis_index[0]
    owners = lax.axis_size(BATCH)
    parts = lax.axis_size("row")
    count = atoms.shape[0]
    slots = (count + owners - 1) // owners
    holding = green.shape[0]
    width = 3 * S * DEG * DEG
    highest = lax.Precision.HIGHEST
    dphi = jnp.einsum("cij,jp->cip", dens, phi, preferred_element_type=jnp.float32)
    phi_wide = phi.astype(jnp.float32)
    density = jnp.sum(phi_wide[None] * dphi, axis=1)
    weighted = measure[None, :] * density
    every_atom = atom_positions.shape[1]
    picked = jnp.arange(every_atom)[:, None] == atoms[None, :]
    centres = jnp.dot(atom_positions, picked.astype(jnp.float32), precision=highest)
    blocks = jnp.sum(jnp.where(picked, shell_blocks[:, None], 0), axis=0)
    group = min(8, count)
    starts = list(range(0, count, group))
    make_tables = jax.vmap(atom_tables, in_axes=(None, 1, 0, None))
    kept = []
    pieces = []
    for first in starts:
        radial, angular = make_tables(
            spots, centres[:, first : first + group], blocks[first : first + group], shell_widths
        )
        kept.append((radial, angular))
        scaled = (radial[:, None] * weighted[None, :, None, :]).astype(jnp.bfloat16)
        pieces.append(
            jnp.einsum("kcsp,klp->kcsl", scaled, angular, preferred_element_type=jnp.float32)
        )
    moments = jnp.concatenate(pieces, axis=0).reshape(count, width)
    home = atoms // holding
    local_slot = atoms % holding
    order = jnp.arange(count)
    before = (home[None, :] == home[:, None]) & (order[None, :] < order[:, None])
    place = home * slots + jnp.sum(before, axis=1)
    routing = jnp.arange(owners * slots)[:, None] == place[None, :]
    outgoing = jnp.dot(routing.astype(jnp.float32), moments, precision=highest).reshape(
        owners, slots, width
    )
    tags = (jnp.sum(jnp.where(routing, local_slot[None, :] + 1, 0), axis=1) - 1).reshape(
        owners, slots
    )
    incoming, sources = (
        lax.all_to_all(outgoing, BATCH, split_axis=0, concat_axis=0, tiled=True),
        lax.all_to_all(tags, BATCH, split_axis=0, concat_axis=0, tiled=True),
    )
    collect = jnp.arange(holding)[:, None] == sources.reshape(1, owners * slots)
    partial_value = jnp.dot(
        collect.astype(jnp.float32), incoming.reshape(owners * slots, width), precision=highest
    )
    totals = of_everyone(partial_value, ("row", "col"))
    potential = apply_green(totals, green)
    back = jnp.dot(
        collect.T.astype(jnp.bfloat16), potential, preferred_element_type=jnp.float32
    ).astype(jnp.bfloat16)
    returned = lax.all_to_all(
        back.reshape(owners, slots, width), BATCH, split_axis=0, concat_axis=0, tiled=True
    )
    tables = jnp.dot(
        routing.T.astype(jnp.bfloat16),
        returned.reshape(owners * slots, width),
        preferred_element_type=jnp.float32,
    )
    tables = tables.astype(jnp.bfloat16).reshape(count, 3, S, DEG * DEG)
    field = jnp.zeros((3, spots.shape[1]), jnp.float32)
    for position, first in enumerate(starts):
        radial, angular = kept[position]
        spread = jnp.einsum(
            "kcsl,klp->kcsp",
            tables[first : first + group],
            angular,
            preferred_element_type=jnp.float32,
        )
        field = field + jnp.einsum("ksp,kcsp->cp", radial, spread, precision=highest)
    piece = labels.shape[0] // parts
    operand = (phi_wide[None] * (measure[None, :] * field)[:, None, :]).astype(jnp.bfloat16)
    quads = jnp.einsum(
        "cxip,yjp->xycij",
        operand.reshape(3, parts, piece, -1),
        phi.reshape(parts, piece, -1),
        preferred_element_type=jnp.float32,
    ).astype(jnp.bfloat16)
    halves = labels.reshape(parts, piece)
    marks = jnp.stack(
        [
            jnp.broadcast_to(halves[:, None, :], (parts, parts, piece)),
            jnp.broadcast_to(halves[None, :, :], (parts, parts, piece)),
        ],
        axis=2,
    )
    got, got_marks = (
        joined_exchange(quads, ("row", "col"), ("row", "col"), (0, 1), (0, 1)),
        joined_exchange(marks, ("row", "col"), ("row", "col"), (0, 1), (0, 1)),
    )
    tile = NB // parts
    row_first = lax.axis_index("row") * tile
    col_first = lax.axis_index("col") * tile
    grid = jnp.arange(tile)
    accum = jnp.zeros((3, tile, tile), jnp.float32)
    for source_row in range(parts):
        for source_col in range(parts):
            rows_hit = (
                grid[:, None] == (got_marks[source_row, source_col, 0] - row_first)[None, :]
            ).astype(jnp.bfloat16)
            cols_hit = (
                grid[:, None] == (got_marks[source_row, source_col, 1] - col_first)[None, :]
            ).astype(jnp.bfloat16)
            placed = jnp.einsum(
                "ti,cij->ctj",
                rows_hit,
                got[source_row, source_col],
                preferred_element_type=jnp.float32,
            ).astype(jnp.bfloat16)
            accum = accum + jnp.einsum(
                "ctj,uj->ctu", placed, cols_hit, preferred_element_type=jnp.float32
            )
    flat = accum.reshape(-1, 128)
    mine = scatter_axes(flat, BATCH, 0).astype(jnp.bfloat16)
    hamiltonian = gathered_by_axis(mine, BATCH, (1, 0, 2), 0).reshape(3, tile, tile)
    return (potential, hamiltonian)


def solution(mesh):
    finer = Mesh(
        mesh.devices.reshape(8, 4, 2, mesh.shape["row"], mesh.shape["col"]),
        ("batch_0", "batch_1", "batch_2", "row", "col"),
    )
    placed = (
        P(BATCH_ROW_COL, None, None),
        P(BATCH_ROW_COL, None, None, None),
        P(BATCH_ROW_COL, None, None),
        P(BATCH_ROW_COL, None),
        P(BATCH_ROW_COL, None),
        P(BATCH_ROW_COL, None),
        P(),
        P(),
        P(),
        P(BATCH, None, None),
    )
    return jax.shard_map(
        on_device,
        mesh=finer,
        in_specs=placed,
        out_specs=(P(BATCH, None), P(None, "row", "col")),
        check_vma=False,
    )
```

profile of v0, /device:TPU:1, one launch (start us, length us, event | category | flops | bytes accessed | tf_op | source)
XLA Modules:
  0.0 514.2 jit_solution(16503074002101347593)
XLA Ops:
  10.2 13.2 %all-to-all-start = ((s32[64,1,1]{2,1,0:T(1,128)}), s32[64,1,1]{2,1,0:T(1,128)}, u32[]{:S(2)}, u32[]{:S(2)}) async-start(s32[64,1,1]{2,1,0:T(1,128)} %copy.66), calls=%async_computation | async-start | bytes 65536 | tf_op jit(solution)/shard_map/all_to_all | solution.py:161
  35.4 7.7 %fusion.70 = (f32[2048,8,64]{0,2,1:T(8,128)}, f32[8,64,2048]{2,1,0:T(8,128)S(1)}, f32[8,64,2048]{2,1,0:T(8,128)S(1)}, f32[2048,8,64]{0,2,1:T(8,128)}, f32[8,64,2...) fusion(f32[64]{0:T(128)} %param.18, ...), kind=kLoop, calls=%fused_computation.83 | loop fusion | flops 20971520 | bytes 33819136
  52.8 2.9 convolution_bitcast_fusion
  55.7 4.9 copy.75
  60.6 10.3 %all-to-all-start.1 = ((f32[64,1,12288]{2,1,0:T(1,128)}), f32[64,1,12288]{2,1,0:T(1,128)S(1)}, u32[]{:S(2)}, u32[]{:S(2)}) async-start(f32[64,1,12288]{2,1,0:T(1,128)} %copy.75), calls=%async_computation.1 | async-start | bytes 6291456 | tf_op jit(solution)/shard_map/all_to_all | solution.py:160
  72.9 70.6 %all-to-all-done.1 = f32[64,1,12288]{2,1,0:T(1,128)S(1)} async-done(((f32[64,1,12288]{2,1,0:T(1,128)}), f32[64,1,12288]{2,1,0:T(1,128)S(1)}, u32[]{:S(2)}, u32[]{:S(2)}) %all-to-all-start.1) | async-done | bytes 3145760 | tf_op jit(solution)/shard_map/all_to_all | solution.py:160
  143.5 2.9 fusion.13
  147.4 4.4 all-to-all-start.2
  153.2 10.6 %all-to-all-done.2 = f32[4,4,12288]{2,1,0:T(4,128)S(1)} async-done(((f32[4,4,12288]{2,1,0:T(4,128)}), f32[4,4,12288]{2,1,0:T(4,128)S(1)}, u32[]{:S(2)}, u32[]{:S(2)}) %all-to-all-start.2) | async-done | bytes 786464 | tf_op jit(solution)/shard_map/all_to_all | solution.py:16
  170.4 2.5 reduce.13
  172.9 4.9 reshape.406
  177.8 7.1 %all-to-all-start.3 = ((bf16[64,2,6144]{2,1,0:T(2,128)(2,1)}), bf16[64,2,6144]{2,1,0:T(2,128)(2,1)}, u32[]{:S(2)}, u32[]{:S(2)}) async-start(bf16[64,2,6144]{2,1,0:T(2,128)(2,1)} %reshape.406), calls=%async_computation.3 | async-start | bytes 3145728 | tf_op jit(solution)/shard_map/all_to_all | solution.py:172
  187.0 36.9 %all-to-all-done.3 = bf16[64,2,6144]{2,1,0:T(2,128)(2,1)} async-done(((bf16[64,2,6144]{2,1,0:T(2,128)(2,1)}), bf16[64,2,6144]{2,1,0:T(2,128)(2,1)}, u32[]{:S(2)}, u32[]{:S(2)}) %all-to-all-start.3) | async-done | bytes 1572896 | tf_op jit(solution)/shard_map/all_to_all | solution.py:172
  223.9 3.5 all-to-all-start.5
  227.4 10.4 %reshape.407 = bf16[64,1,12288]{2,1,0:T(2,128)(2,1)} reshape(bf16[64,2,6144]{2,1,0:T(2,128)(2,1)} %all-to-all-done.3) | data formatting | bytes 3145728
  237.7 3.8 convolution_convert_fusion.1
  244.7 4.0 multiply_reduce_fusion
  257.3 4.2 all-to-all-start.4
  261.9 5.1 all-to-all-done.4
  267.1 4.3 fusion.58
  271.4 4.3 fusion.54
  275.7 4.4 fusion.56
  280.1 11.2 %add_add_fusion = f32[3,768,768]{2,1,0:T(8,128)} fusion(f32[3,768,768]{2,1,0:T(8,128)} %fusion.58, f32[3,768,768]{2,1,0:T(8,128)} %fusion.54, f32[3,768,768]{2,1,0:T(8,128)} %fusion.56, s32[96]{0:T(128)S(1)} %get-tuple-element.47, s32[96]{0:T(128)S(1)} %get-tuple-element.46, bf16[2,2,3,96,96]{3,4,2,1,0:T(8,128)(2,1)S(1)} %bitcast.238), kind=kOutput, calls=%fused_computation.12 | convolution fusion | flops 387883008 | bytes 28386304 | tf_op jit(solution)/shard_map/ctj,uj->ctu/dot_general | solution.py:230
  291.3 8.2 %reshape.367 = f32[13824,128]{1,0:T(8,128)} reshape(f32[3,768,768]{2,1,0:T(8,128)} %add_add_fusion) | data formatting | bytes 14155776 | tf_op jit(solution)/shard_map/reshape | solution.py:233
  299.6 79.9 %reduce-scatter.7.cloned.1.call-done = f32[1728,128]{1,0:T(8,128)} async-done(((f32[13824,128]{1,0:T(8,128)}), f32[1728,128]{1,0:T(8,128)}) %reduce-scatter.7.cloned.1.call-update) | async-done | bytes 884752 | tf_op jit(solution)/shard_map/reduce_scatter | solution.py:50
  379.6 25.1 %reduce-scatter.9.cloned.1.call-done = f32[432,128]{1,0:T(8,128)} async-done(((f32[1728,128]{1,0:T(8,128)}), f32[432,128]{1,0:T(8,128)}) %reduce-scatter.9.cloned.1.call-update) | async-done | bytes 221200 | tf_op jit(solution)/shard_map/reduce_scatter | solution.py:50
  404.8 17.2 %reduce-scatter.11.cloned.1.call-done = f32[216,128]{1,0:T(8,128)} async-done(((f32[432,128]{1,0:T(8,128)}), f32[216,128]{1,0:T(8,128)}) %reduce-scatter.11.cloned.1.call-update) | async-done | bytes 110608
  422.9 10.1 %all-gather = bf16[864,128]{1,0:T(8,128)(2,1)} all-gather(bf16[216,128]{1,0:T(8,128)(2,1)S(1)} %convert_element_type.160), channel_id=2, replica_groups=mesh['batch_0'=8,'batch_1'=4,'batch_2'=2,'row'=2,'col'=2] {'batch_1'}, dimensions={0}, use_global_device_ids=true | all-gather | bytes 276480 | tf_op jit(solution)/shard_map/all_gather | solution.py:57
  433.0 39.8 %all-gather.4.cloned.1.call-done = bf16[32,216,128]{2,1,0:T(8,128)(2,1)} async-done(((bf16[4,216,128]{2,1,0:T(8,128)(2,1)}), bf16[32,216,128]{2,1,0:T(8,128)(2,1)}) %all-gather.4.cloned.1.call-update) | async-done | bytes 1769488 | tf_op jit(solution)/shard_map/all_gather | solution.py:57
  472.8 22.9 %all-gather.6.cloned.1.call-done = bf16[64,216,128]{2,1,0:T(8,128)(2,1)} async-done(((bf16[32,216,128]{2,1,0:T(8,128)(2,1)}), bf16[64,216,128]{2,1,0:T(8,128)(2,1)}) %all-gather.6.cloned.1.call-update) | async-done | bytes 3538960 | tf_op jit(solution)/shard_map/all_gather | solution.py:57
  495.8 4.1 copy.81
  499.9 7.3 %reshape_reshape_reshape.3 = bf16[3,768,768]{2,1,0:T(8,128)(2,1)} reshape(bf16[8,4,2,216,128]{4,3,2,1,0:T(8,128)(2,1)} %copy.81) | data formatting | bytes 7077888 | tf_op jit(solution)/shard_map/reshape;reshape;reshape | solution.py:235
  (185 shorter events, 50.4 us)
Async XLA Ops:
  7.2 27.4 %copy-start = (bf16[1,3,192,192]{3,2,1,0:T(8,128)(2,1)S(1)}, bf16[1,3,192,192]{3,2,1,0:T(8,128)(2,1)}, u32[]{:S(2)}) copy-start(bf16[1,3,192,192]{3,2,1,0:T(8,128)(2,1)} %param.11) | copy-start | bytes 663556
  10.2 50.5 %all-to-all-start = ((s32[64,1,1]{2,1,0:T(1,128)}), s32[64,1,1]{2,1,0:T(1,128)}, u32[]{:S(2)}, u32[]{:S(2)}) async-start(s32[64,1,1]{2,1,0:T(1,128)} %copy.66), calls=%async_computation | async-start | bytes 65536 | tf_op jit(solution)/shard_map/all_to_all | solution.py:161
  29.1 14.0 %copy-start.7 = (f32[8,8,2048]{2,1,0:T(8,128)}, f32[8,8,2048]{2,1,0:T(8,128)S(1)}, u32[]{:S(2)}) copy-start(f32[8,8,2048]{2,1,0:T(8,128)S(1)} %copy.74) | copy-start | bytes 1572868
  29.4 13.6 %copy-start.8 = (f32[8,8,2048]{2,1,0:T(8,128)}, f32[8,8,2048]{2,1,0:T(8,128)S(1)}, u32[]{:S(2)}) copy-start(f32[8,8,2048]{2,1,0:T(8,128)S(1)} %copy.73) | copy-start | bytes 1572868
  30.1 14.8 %copy-start.9 = (f32[8,8,2048]{2,1,0:T(8,128)}, f32[8,8,2048]{2,1,0:T(8,128)S(1)}, u32[]{:S(2)}) copy-start(f32[8,8,2048]{2,1,0:T(8,128)S(1)} %copy.72) | copy-start | bytes 1572868
  30.4 14.5 %copy-start.11 = (f32[8,8,2048]{2,1,0:T(8,128)}, f32[8,8,2048]{2,1,0:T(8,128)S(1)}, u32[]{:S(2)}) copy-start(f32[8,8,2048]{2,1,0:T(8,128)S(1)} %copy.71) | copy-start | bytes 1572868
  30.4 4.1 copy-start.2
  31.1 15.6 %copy-start.13 = (f32[8,8,2048]{2,1,0:T(8,128)}, f32[8,8,2048]{2,1,0:T(8,128)S(1)}, u32[]{:S(2)}) copy-start(f32[8,8,2048]{2,1,0:T(8,128)S(1)} %copy.70) | copy-start | bytes 1572868
  31.4 15.3 %copy-start.15 = (f32[8,8,2048]{2,1,0:T(8,128)}, f32[8,8,2048]{2,1,0:T(8,128)S(1)}, u32[]{:S(2)}) copy-start(f32[8,8,2048]{2,1,0:T(8,128)S(1)} %copy.69) | copy-start | bytes 1572868
  31.4 3.9 copy-start.23
  32.1 16.5 %copy-start.17 = (f32[8,8,2048]{2,1,0:T(8,128)}, f32[8,8,2048]{2,1,0:T(8,128)S(1)}, u32[]{:S(2)}) copy-start(f32[8,8,2048]{2,1,0:T(8,128)S(1)} %copy.68) | copy-start | bytes 1572868
  50.4 2.4 copy-start.25
  60.6 82.9 %all-to-all-start.1 = ((f32[64,1,12288]{2,1,0:T(1,128)}), f32[64,1,12288]{2,1,0:T(1,128)S(1)}, u32[]{:S(2)}, u32[]{:S(2)}) async-start(f32[64,1,12288]{2,1,0:T(1,128)} %copy.75), calls=%async_computation.1 | async-start | bytes 6291456 | tf_op jit(solution)/shard_map/all_to_all | solution.py:160
  147.4 16.5 %all-to-all-start.2 = ((f32[4,4,12288]{2,1,0:T(4,128)}), f32[4,4,12288]{2,1,0:T(4,128)S(1)}, u32[]{:S(2)}, u32[]{:S(2)}) async-start(f32[4,4,12288]{2,1,0:T(4,128)} %broadcast_in_dim.66), calls=%async_computation.2 | async-start | bytes 1572864 | tf_op jit(solution)/shard_map/all_to_all | solution.py:16
  169.2 8.6 %copy-start.21 = (bf16[4,12288]{1,0:T(4,128)(2,1)}, bf16[4,12288]{1,0:T(4,128)(2,1)S(1)}, u32[]{:S(2)}) copy-start(bf16[4,12288]{1,0:T(4,128)(2,1)S(1)} %reshape.358) | copy-start | bytes 294916
  170.4 15.0 %copy-start.26 = (s32[1,192]{1,0:T(1,128)S(1)}, s32[1,192]{1,0:T(1,128)}, u32[]{:S(2)}) copy-start(s32[1,192]{1,0:T(1,128)} %param.15) | copy-start | bytes 2308
  170.4 15.8 %copy-start.3 = (bf16[1,192,2048]{2,1,0:T(8,128)(2,1)S(1)}, bf16[1,192,2048]{2,1,0:T(8,128)(2,1)}, u32[]{:S(2)}) copy-start(bf16[1,192,2048]{2,1,0:T(8,128)(2,1)} %param.10) | copy-start | bytes 2359300
  177.8 46.0 %all-to-all-start.3 = ((bf16[64,2,6144]{2,1,0:T(2,128)(2,1)}), bf16[64,2,6144]{2,1,0:T(2,128)(2,1)}, u32[]{:S(2)}, u32[]{:S(2)}) async-start(bf16[64,2,6144]{2,1,0:T(2,128)(2,1)} %reshape.406), calls=%async_computation.3 | async-start | bytes 3145728 | tf_op jit(solution)/shard_map/all_to_all | solution.py:172
  223.9 33.5 %all-to-all-start.5 = ((s32[4,1,1,2,96]{4,3,2,1,0:T(2,128)}), s32[4,1,1,2,96]{4,3,2,1,0:T(2,128)S(1)}, u32[]{:S(2)}, u32[]{:S(2)}) async-start(s32[4,1,1,2,96]{4,3,2,1,0:T(2,128)} %bitcast.63), calls=%async_computation.5 | async-start | bytes 8192 | tf_op jit(solution)/shard_map/all_to_all | solution.py:42
  244.6 4.1 copy-start.6
  244.6 4.1 copy-start.10
  244.6 4.1 copy-start.12
  244.7 4.2 copy-start.22
  248.9 2.5 copy-start.20
  251.3 2.5 copy-start.16
  257.3 9.6 %all-to-all-start.4 = ((bf16[4,1,1,3,96,96]{5,4,3,2,1,0:T(8,128)(2,1)}), bf16[4,1,1,3,96,96]{5,4,3,2,1,0:T(8,128)(2,1)S(1)}, u32[]{:S(2)}, u32[]{:S(2)}) async-start(bf16[4,1,1,3,96,96]{5,4,3,2,1,0:T(8,128)(2,1)} %copy.79), calls=%async_computation.4 | async-start | bytes 589824 | tf_op jit(solution)/shard_map/all_to_all | solution.py:42
  261.6 118.0 %reduce-scatter.7.cloned.1.call-start = ((), (), s32[]{:S(2)}) async-start(), calls=%async_computation.9 | async-start | bytes 7962624 | tf_op jit(solution)/shard_map/reduce_scatter | solution.py:50
  299.5 105.2 %reduce-scatter.9.cloned.1.call-start = ((), (), s32[]{:S(2)}) async-start(), calls=%async_computation.10 | async-start | bytes 1105920 | tf_op jit(solution)/shard_map/reduce_scatter | solution.py:50
  379.6 42.4 %reduce-scatter.11.cloned.1.call-start = ((), (), s32[]{:S(2)}) async-start(), calls=%async_computation.13 | async-start | bytes 331776
  404.8 68.1 %all-gather.4.cloned.1.call-start = ((), (), s32[]{:S(2)}) async-start(), calls=%async_computation.11 | async-start | bytes 1990656 | tf_op jit(solution)/shard_map/all_gather | solution.py:57
  433.0 62.8 %all-gather.6.cloned.1.call-start = ((), (), s32[]{:S(2)}) async-start(), calls=%async_computation.12 | async-start | bytes 5308416 | tf_op jit(solution)/shard_map/all_gather | solution.py:57
  495.8 11.4 %copy-start.1 = (bf16[1,3,192,192]{3,2,1,0:T(8,128)(2,1)S(1)}, bf16[1,3,192,192]{3,2,1,0:T(8,128)(2,1)}, u32[]{:S(2)}) copy-start(bf16[1,3,192,192]{3,2,1,0:T(8,128)(2,1)} %param.11) | copy-start | bytes 663556
  (6 other events, 11.4 us)
Sparse Core Ops, SparseCore 0:
  299.7 79.8 reduce-scatter.6
  382.1 22.5 reduce-scatter.8
  407.2 14.6 reduce-scatter.10
  433.1 39.6 all-gather.3
  474.5 21.2 all-gather.5
where the time goes:
time: 521 us; the launch traced here: 514 us
  waiting for transfers between devices  308 us (59%)
  local copies, waits for them, and re-layouts  60.8 us (12%)
  matrix products  54.6 us (10%)
  starting transfers between devices  43.1 us (8%)
  other arithmetic  22.2 us (4%)
  between operations  15.3 us (3%)
  blocking collectives  10.1 us (2%)
    reduce_scatter x2, waiting for transfers between devices, scatter_axes(): nearer = lax.psum_scatter(x, axes[0], scatter_dimension=dim, tiled=True)  105 us
    all_to_all x1, waiting for transfers between devices, on_device(): lax.all_to_all(outgoing, BATCH, split_axis=0, concat_axis=0, tiled=True)  70.6 us
    all_gather x2, waiting for transfers between devices, gather_in_order(): parts = lax.all_gather(parts, axes[k], axis=0, tiled=True)  62.7 us
    all_to_all x1, waiting for transfers between devices, on_device(): lax.all_to_all(back.reshape(owners, slots, width), BATCH, split_axis=0, c...  36.9 us
    dot_general x4, matrix products, on_device(): jnp.einsum('ctj,uj->ctu', placed, cols_hit, preferred_element_type=jnp.fl...  24.1 us
    unnamed x70, local copies, waits for them, and re-layouts  18.4 us
    unnamed x6, waiting for transfers between devices  17.3 us
    all_to_all x1, starting transfers between devices, on_device(): lax.all_to_all(tags, BATCH, split_axis=0, concat_axis=0, tiled=True)  13.2 us
  transfers between devices with their start and end apart: 11, of which 9 were waited for; matrix products, arithmetic and copies ran while one was open for 14% of the time, Pallas kernels for 0%

commit v1 on v0

v1 whole, which is shorter than its diff:
```python
import math

import jax
import jax.numpy as jnp
from jax import lax
from jax.experimental import pallas as pl
from jax.experimental.pallas import tpu as pltpu
from jax.sharding import Mesh
from jax.sharding import PartitionSpec as P

S = 64
DEG = 8
L = 64
NB = 1536
BATCH = ("batch_0", "batch_1", "batch_2")
BATCH_ROW_COL = ("batch_0", "batch_1", "batch_2", "row", "col")
MESH = pl.DeviceIdType.MESH
F32 = jnp.float32
BF16 = jnp.bfloat16
HALF_S = S // 2
VMEM_LIMIT = 56 * 1024 * 1024
NT = (((1,), (1,)), ((), ()))


def vmem():
    return pl.BlockSpec(memory_space=pltpu.VMEM)


def smem():
    return pl.BlockSpec(memory_space=pltpu.SMEM)


def fill_rows(atoms_ref, pos_ref, pts_ref, dist_ref, polar_ref, side_ref):
    count = atoms_ref.shape[0]
    every = pos_ref.shape[1]
    picked = lax.broadcasted_iota(jnp.int32, (count, every), 1) == atoms_ref[...]
    centre = [
        jnp.sum(jnp.where(picked, pos_ref[d : d + 1, :], 0.0), axis=1, keepdims=True)
        for d in range(3)
    ]
    for group in range(count // 8):
        rows = slice(group * 8, group * 8 + 8)
        dx, dy, dz = [pts_ref[d : d + 1, :] - centre[d][rows] for d in range(3)]
        dist = jnp.sqrt(dx * dx + dy * dy + dz * dz + 0.01)
        inverse = 1.0 / dist
        dist_ref[group] = dist
        for value, ref in ((dz * inverse, polar_ref), (dx * inverse, side_ref)):
            older, newer = jnp.ones_like(value), value
            ref[0, group] = older
            ref[1, group] = newer
            for order in range(2, DEG):
                older, newer = newer, 2.0 * value * newer - older
                ref[order, group] = newer


def shell_rows(widths_ref, lanes):
    row = lax.broadcasted_iota(jnp.int32, (S, lanes), 0)
    shell = jnp.where(row < HALF_S, 2 * row, 2 * (row - HALF_S) + 1)
    middle = shell.astype(F32) * (4.0 / S)
    scale = math.sqrt(math.log2(math.e)) / widths_ref[...]
    return shell, middle, scale


def radial_of(dist, middle, scale, live):
    t = (dist - middle) * scale
    return jnp.where(live, jnp.exp2(-(t * t)), 0.0)


def angular_of(polar_ref, side_ref, group, u, cols):
    side = jnp.concatenate([side_ref[j, group, u : u + 1, cols] for j in range(DEG)], axis=0)
    return jnp.concatenate(
        [side * polar_ref[i, group, u : u + 1, cols] for i in range(DEG)], axis=0
    ).astype(BF16)


def moments_kernel(
    atoms_s, blocks_s, atoms_ref, pos_ref, pts_ref, w_ref, widths_ref, phi_ref, dens_ref,
    out_ref, dist_ref, polar_ref, side_ref, wd_ref, scaled_ref, ang_ref, mid_ref, inv_ref,
):
    count = atoms_ref.shape[0]
    points = phi_ref.shape[1]
    fill_rows(atoms_ref, pos_ref, pts_ref, dist_ref, polar_ref, side_ref)
    wide = min(512, points)
    for first in range(0, points, wide):
        cols = slice(first, first + wide)
        phi = phi_ref[:, cols]
        for c in range(3):
            dphi = jnp.dot(dens_ref[c], phi, preferred_element_type=F32)
            total = jnp.sum(phi.astype(F32) * dphi, axis=0, keepdims=True)
            wd_ref[c : c + 1, cols] = total * w_ref[:, cols]
    shell, middle, scale = shell_rows(widths_ref, 128)
    mid_ref[...] = middle
    inv_ref[...] = scale
    out_ref[count] = jnp.zeros((3 * HALF_S, 2 * L), BF16)

    def eight(group, carry):
        for u in range(8):
            k = group * 8 + u
            b = u % 2
            live = shell < 8 * blocks_s[atoms_s[0, k]]
            for first in range(0, points, 128):
                cols = slice(first, first + 128)
                rad = radial_of(dist_ref[group, u : u + 1, cols], mid_ref[...], inv_ref[...], live)
                for c in range(3):
                    part = (rad * wd_ref[c : c + 1, cols]).astype(BF16)
                    for par in range(2):
                        row = par * 96 + c * HALF_S
                        scaled_ref[b, row : row + HALF_S, cols] = part[
                            par * HALF_S : (par + 1) * HALF_S
                        ]
                ang_ref[b, :, cols] = angular_of(polar_ref, side_ref, group, u, cols)
            got = lax.dot_general(scaled_ref[b], ang_ref[b], NT, preferred_element_type=F32)
            out_ref[k] = jnp.concatenate([got[:96], got[96:]], axis=1).astype(BF16)
        return carry

    lax.fori_loop(0, count // 8, eight, 0)


def moments_call(atoms, blocks, atoms_col, pos, pts, w, widths, phi, dens):
    count = atoms.shape[1]
    points = phi.shape[1]
    return pl.pallas_call(
        moments_kernel,
        out_shape=jax.ShapeDtypeStruct((count + 1, 96, 128), BF16),
        in_specs=[smem(), smem()] + [vmem()] * 7,
        out_specs=vmem(),
        scratch_shapes=[
            pltpu.VMEM((count // 8, 8, points), F32),
            pltpu.VMEM((DEG, count // 8, 8, points), F32),
            pltpu.VMEM((DEG, count // 8, 8, points), F32),
            pltpu.VMEM((8, points), F32),
            pltpu.VMEM((2, 192, points), BF16),
            pltpu.VMEM((2, L, points), BF16),
            pltpu.VMEM((S, 128), F32),
            pltpu.VMEM((S, 128), F32),
        ],
        compiler_params=pltpu.CompilerParams(vmem_limit_bytes=VMEM_LIMIT),
        cost_estimate=pl.CostEstimate(flops=4_000_000_000, bytes_accessed=3_000_000, transcendentals=4_000_000),
        name="moments",
    )(atoms, blocks, atoms_col, pos, pts, w, widths, phi, dens)


class Rings:
    def __init__(self, send, recv):
        self.send, self.recv = send, recv
        self.used = 0
        self.started = []
        self.core = lax.axis_index("batch_2")
        self.turn = 1 - 2 * self.core
        rows = lax.axis_size("row")
        self.size = {
            "z": lax.axis_size("batch_0"),
            "x": lax.axis_size("batch_1"),
            "y": rows * lax.axis_size("col"),
        }
        self.at = {
            "z": lax.axis_index("batch_0"),
            "x": lax.axis_index("batch_1"),
            "y": lax.axis_index("col") * rows + lax.axis_index("row"),
        }

    def place(self, axis, shift):
        n = self.size[axis]
        return lax.rem(self.at[axis] + shift + 2 * n, n)

    def device(self, axis, shift):
        spot = self.place(axis, shift)
        if axis == "z":
            return {"batch_0": spot}
        if axis == "x":
            return {"batch_1": spot}
        rows = lax.axis_size("row")
        return {"row": lax.rem(spot, rows), "col": spot // rows}

    def sibling(self):
        return {"batch_2": 1 - self.core}

    def greet(self, axes, others=()):
        barrier = pltpu.get_barrier_semaphore()
        greeted = 0
        for axis in axes:
            if self.size[axis] > 1:
                for shift in (1, -1):
                    pl.semaphore_signal(
                        barrier, inc=1, device_id=self.device(axis, shift), device_id_type=MESH
                    )
                    greeted += 1
        for other in others:
            pl.semaphore_signal(barrier, inc=1, device_id=other, device_id_type=MESH)
            greeted += 1
        pl.semaphore_wait(barrier, greeted)

    def ticket(self):
        self.used += 1
        return self.used - 1

    def copy(self, src, dst, ticket, device):
        made = pltpu.make_async_remote_copy(
            src_ref=src, dst_ref=dst, send_sem=self.send.at[ticket],
            recv_sem=self.recv.at[ticket], device_id=device, device_id_type=MESH,
        )
        made.start()
        self.started.append(made)

    def arrive(self, dst, ticket):
        pltpu.make_async_remote_copy(
            src_ref=dst, dst_ref=dst, send_sem=self.send.at[ticket],
            recv_sem=self.recv.at[ticket], device_id=self.sibling(), device_id_type=MESH,
        ).wait_recv()

    def finish(self):
        for made in self.started:
            made.wait_send()

    def reduce(self, buf, base, rows, axis, slots, spot):
        n = self.size[axis]
        if n == 1:
            return
        here = self.at[axis]
        lanes = [(1, n // 2), (-1, n // 2 - 1)]
        tickets = [[self.ticket() for _ in range(steps)] for _, steps in lanes]
        places = []
        for _, steps in lanes:
            places.append([spot + rows * k for k in range(steps)])
            spot += rows * steps

        def own(shift):
            return pl.ds(pl.multiple_of(base + self.place(axis, shift) * rows, 16), rows)

        for t in range(n // 2):
            for lane, (way, steps) in enumerate(lanes):
                if t >= steps:
                    continue
                mine = own(-way * self.turn * (steps - t))
                if t == 0:
                    source = buf.at[mine]
                else:
                    source = slots.at[pl.ds(places[lane][t - 1], rows)]
                    yield
                    self.arrive(source, tickets[lane][t - 1])
                    source[...] = (source[...].astype(F32) + buf[mine, :].astype(F32)).astype(BF16)
                self.copy(
                    source, slots.at[pl.ds(places[lane][t], rows)], tickets[lane][t],
                    self.device(axis, -way * self.turn),
                )
        total = buf[own(0), :].astype(F32)
        for lane, (way, steps) in enumerate(lanes):
            if steps:
                source = slots.at[pl.ds(places[lane][-1], rows)]
                yield
                self.arrive(source, tickets[lane][-1])
                total = total + source[...].astype(F32)
        buf[own(0), :] = total.astype(BF16)

    def gather(self, buf, base, rows, axis, arrived=None):
        n = self.size[axis]
        if arrived:
            arrived(0)
        if n == 1:
            return
        lanes = [(1, n // 2), (-1, n // 2 - 1)]
        tickets = [[self.ticket() for _ in range(steps)] for _, steps in lanes]

        def chunk(shift):
            start = pl.multiple_of(base + self.place(axis, shift) * rows, 16)
            return buf.at[pl.ds(start, rows)]

        for t in range(n // 2 + 1):
            for lane, (way, steps) in enumerate(lanes):
                if t > steps or steps == 0:
                    continue
                block = chunk(way * self.turn * t)
                if t > 0:
                    yield
                    self.arrive(block, tickets[lane][t - 1])
                if t < steps:
                    self.copy(block, block, tickets[lane][t], self.device(axis, -way * self.turn))
                if t > 0 and arrived:
                    arrived(way * t)


def run_together(tasks):
    tasks = list(tasks)
    while tasks:
        for task in list(tasks):
            try:
                next(task)
            except StopIteration:
                tasks.remove(task)


def spread_out(rings, tab, base, total_rows, axes, forwards):
    mine = tab.at[rings.core]
    levels = []
    rows, start = total_rows, base
    for axis in axes:
        rows //= rings.size[axis]
        levels.append((axis, start, rows))
        start = start + rings.at[axis] * rows
    for depth in reversed(range(len(levels))):
        axis, first, rows = levels[depth]

        def forward(shift, axis=axis, first=first, rows=rows):
            ticket = rings.ticket()
            signed = shift * rings.turn
            here = pl.ds(pl.multiple_of(first + rings.place(axis, signed) * rows, 16), rows)
            there = pl.ds(pl.multiple_of(first + rings.place(axis, -signed) * rows, 16), rows)
            rings.copy(tab.at[rings.core, here], tab.at[rings.core, here], ticket, rings.sibling())
            forwards.append((tab.at[1 - rings.core, there], ticket))

        yield from rings.gather(mine, first, rows, axis, forward if depth == 0 else None)


def collect(rings, buf, base, total_rows, axes, slots, spot):
    rows, start = total_rows, base
    for axis in axes:
        rows //= rings.size[axis]
        yield from rings.reduce(buf, start, rows, axis, slots, spot)
        spot += rows * (rings.size[axis] - 1)
        start = start + rings.at[axis] * rows


def chunk_start(rings, base, total_rows, axes):
    rows, start = total_rows, base
    for axis in axes:
        rows //= rings.size[axis]
        start = start + rings.at[axis] * rows
    return start, rows


ATOM_ORDERS = (("y", "x", "z"), ("z", "y", "x"), ("x", "z", "y"))


def atoms_kernel(
    own_s, sib_s, mom_ref, green_ref, tab_ref, pot_ref, dense, slots, other, send, recv
):
    rings = Rings(send, recv)
    nz, nx, ny = (rings.size[a] for a in "zxy")
    held = nz * nx * ny
    part_rows = held * HALF_S
    rings.greet("zxy", [rings.sibling()])
    ticket = rings.ticket()
    rings.copy(mom_ref, other, ticket, rings.sibling())
    rings.arrive(other, ticket)

    def place(slot, order):
        spots = {"z": slot // (nx * ny), "x": lax.rem(slot // ny, nx), "y": lax.rem(slot, ny)}
        index = 0
        for axis in order:
            index = index * rings.size[axis] + spots[axis]
        return index

    def fill(slot, carry):
        value = mom_ref[own_s[0, slot]] + other[sib_s[0, slot]]
        for part, order in enumerate(ATOM_ORDERS):
            row = pl.multiple_of(part * part_rows + place(slot, order) * HALF_S, 32)
            dense[pl.ds(row, HALF_S), :] = value[part * HALF_S : (part + 1) * HALF_S]
        return carry

    lax.fori_loop(0, held, fill, 0)
    forwards = []
    green = green_ref[...]
    column = lax.broadcasted_iota(jnp.int32, (DEG, HALF_S, L), 2) // DEG
    layer = lax.broadcasted_iota(jnp.int32, (DEG, HALF_S, L), 0)

    def task(part):
        order = ATOM_ORDERS[part]
        base = part * part_rows
        yield from collect(rings, dense, base, part_rows, order, slots, base)
        start, rows = chunk_start(rings, base, part_rows, order)
        here = pl.ds(pl.multiple_of(start, 32), rows)
        charges = dense[here, :].astype(F32)
        stacked = jnp.concatenate([charges[:, :L], charges[:, L:]], axis=0).astype(BF16)
        result = jnp.dot(green, stacked, preferred_element_type=F32)
        sides = []
        for par in range(2):
            block = result[par * DEG * HALF_S : (par + 1) * DEG * HALF_S].reshape(DEG, HALF_S, L)
            sides.append(jnp.sum(jnp.where(column == layer, block, 0.0), axis=0))
        tab_ref[rings.core, here, :] = jnp.concatenate(sides, axis=1).astype(BF16)
        yield from spread_out(rings, tab_ref, base, part_rows, order, forwards)

    run_together(task(part) for part in range(3))
    for slot in range(ny):
        for part, order in enumerate(ATOM_ORDERS):
            index = 0
            for axis in order:
                index = index * rings.size[axis] + (slot if axis == "y" else rings.at[axis])
            row = pl.multiple_of(part * part_rows + index * HALF_S, 32)
            pot_ref[slot, part * HALF_S : (part + 1) * HALF_S, :] = tab_ref[
                rings.core, pl.ds(row, HALF_S), :
            ]
    for block, ticket in forwards:
        rings.arrive(block, ticket)
    rings.finish()


def atoms_call(own, sib, moments, green, planes):
    held = own.shape[1]
    return pl.pallas_call(
        atoms_kernel,
        out_shape=(
            jax.ShapeDtypeStruct((2, 3 * held * HALF_S, 128), BF16),
            jax.ShapeDtypeStruct((planes, 96, 128), BF16),
        ),
        in_specs=[smem(), smem(), vmem(), vmem()],
        out_specs=(vmem(), vmem()),
        scratch_shapes=[
            pltpu.VMEM((3 * held * HALF_S, 128), BF16),
            pltpu.VMEM((3 * held * HALF_S, 128), BF16),
            pltpu.VMEM(moments.shape, BF16),
            pltpu.SemaphoreType.DMA((112,)),
            pltpu.SemaphoreType.DMA((112,)),
        ],
        compiler_params=pltpu.CompilerParams(
            vmem_limit_bytes=VMEM_LIMIT, collective_id=0, has_side_effects=True
        ),
        cost_estimate=pl.CostEstimate(flops=100_000_000, bytes_accessed=60_000_000, transcendentals=0),
        name="atoms",
    )(own, sib, moments, green)


def field_kernel(
    rows_s, atoms_s, blocks_s, atoms_ref, pos_ref, pts_ref, w_ref, widths_ref, phi_ref, tab_ref,
    out_ref, dist_ref, polar_ref, side_ref, acc_ref, operand_ref, pad_ref, mid_ref, inv_ref,
):
    count = atoms_ref.shape[0]
    points = phi_ref.shape[1]
    basis = phi_ref.shape[0]
    piece = basis // 2
    fill_rows(atoms_ref, pos_ref, pts_ref, dist_ref, polar_ref, side_ref)
    wide = min(256, points)
    shell, middle, scale = shell_rows(widths_ref, wide)
    mid_ref[...] = middle
    inv_ref[...] = scale
    acc_ref[...] = jnp.zeros_like(acc_ref)

    def eight(group, carry):
        for u in range(8):
            k = group * 8 + u
            live = shell < 8 * blocks_s[atoms_s[0, k]]
            packed = [
                tab_ref[pl.ds(pl.multiple_of(rows_s[c, k], 32), HALF_S), :] for c in range(3)
            ]
            packed = jnp.concatenate(packed, axis=0)
            table = jnp.concatenate([packed[:, :L], packed[:, L:]], axis=0)
            for first in range(0, points, wide):
                cols = slice(first, first + wide)
                ang = angular_of(polar_ref, side_ref, group, u, cols)
                spread = jnp.dot(table, ang, preferred_element_type=F32)
                rad = radial_of(dist_ref[group, u : u + 1, cols], mid_ref[...], inv_ref[...], live)
                for c in range(3):
                    total = acc_ref[c, :, cols]
                    for par in range(2):
                        row = par * 96 + c * HALF_S
                        prod = spread[row : row + HALF_S] * rad[par * HALF_S : (par + 1) * HALF_S]
                        for g in range(0, HALF_S, 8):
                            total = total + prod[g : g + 8]
                    acc_ref[c, :, cols] = total
        return carry

    lax.fori_loop(0, count // 8, eight, 0)
    for q in range(2):
        pad_ref[q, :piece, :] = phi_ref[q * piece : (q + 1) * piece, :]
        pad_ref[q, piece:, :] = jnp.zeros((128 - piece, points), BF16)
    for c in range(3):
        field = jnp.sum(acc_ref[c], axis=0, keepdims=True) * w_ref[...]
        for first in range(0, points, wide):
            cols = slice(first, first + wide)
            operand_ref[:, cols] = (phi_ref[:, cols].astype(F32) * field[:, cols]).astype(BF16)
        for q in range(2):
            local = lax.dot_general(
                operand_ref[...], pad_ref[q], NT, preferred_element_type=F32
            ).astype(BF16)
            for r in range(2):
                out_ref[r * 2 + q, :, c * 128 : (c + 1) * 128] = local[r * piece : (r + 1) * piece]


def field_call(rows, atoms, blocks, atoms_col, pos, pts, w, widths, phi, tab):
    count = atoms.shape[1]
    basis, points = phi.shape
    wide = min(256, points)
    return pl.pallas_call(
        field_kernel,
        out_shape=jax.ShapeDtypeStruct((4, basis // 2, 384), BF16),
        in_specs=[smem()] * 3 + [vmem()] * 7,
        out_specs=vmem(),
        scratch_shapes=[
            pltpu.VMEM((count // 8, 8, points), F32),
            pltpu.VMEM((DEG, count // 8, 8, points), F32),
            pltpu.VMEM((DEG, count // 8, 8, points), F32),
            pltpu.VMEM((3, 8, points), F32),
            pltpu.VMEM((basis, points), BF16),
            pltpu.VMEM((2, 128, points), BF16),
            pltpu.VMEM((S, wide), F32),
            pltpu.VMEM((S, wide), F32),
        ],
        compiler_params=pltpu.CompilerParams(vmem_limit_bytes=VMEM_LIMIT),
        cost_estimate=pl.CostEstimate(flops=4_000_000_000, bytes_accessed=8_000_000, transcendentals=4_000_000),
        name="field",
    )(rows, atoms, blocks, atoms_col, pos, pts, w, jnp.broadcast_to(widths[:, :1], (S, wide)), phi, tab)


TILE_ORDERS = (("z", "x"), ("x", "z"))


def matrix_kernel(quads_ref, label_ref, tab_ref, flat, slots, got, marks, placed, hit, send, recv):
    rings = Rings(send, recv)
    row, col, core = (lax.axis_index(a) for a in ("row", "col", "batch_2"))
    n_row, n_col = lax.axis_size("row"), lax.axis_size("col")
    piece = quads_ref.shape[1]
    tile = hit.shape[0]
    half = tile // 2
    me = (core * n_row + row) * n_col + col
    shifts = [
        (dc, dr, dl) for dc in range(2) for dr in range(n_row) for dl in range(n_col)
    ][1:]

    def peer(shift):
        return {
            "batch_2": lax.rem(core + shift[0], 2),
            "row": lax.rem(row + shift[1], n_row),
            "col": lax.rem(col + shift[2], n_col),
        }

    rings.greet("zx", [peer(shift) for shift in shifts])
    waits = []
    for shift in shifts:
        to = peer(shift)
        first, second = rings.ticket(), rings.ticket()
        rings.copy(label_ref, marks.at[me], first, to)
        rings.copy(quads_ref.at[to["row"] * 2 + to["col"]], got.at[me], second, to)
        source = (to["batch_2"] * n_row + to["row"]) * n_col + to["col"]
        waits.append((marks.at[source], first, got.at[source], second))
    marks[me] = label_ref[...]
    got[me] = quads_ref[row * 2 + col]
    padded = flat.shape[0] - 3 * half * (tile // 128)
    flat[flat.shape[0] - padded :, :] = jnp.zeros((padded, 128), BF16)
    for mark, first, block, second in waits:
        rings.arrive(mark, first)
        rings.arrive(block, second)
    sources = 2 * n_row * n_col
    for s in range(sources):
        label = marks[s]
        rows_at = jnp.where(row == 0, label[0:1, :], label[1:2, :]) - row * tile - core * half
        cols_at = jnp.where(col == 0, label[0:1, :], label[1:2, :]) - col * tile
        row_hit = lax.broadcasted_iota(jnp.int32, (half, 128), 0) == rows_at
        row_hit = jnp.where(row_hit, 1.0, 0.0).astype(BF16)[:, :piece]
        spread = jnp.dot(row_hit, got[s], preferred_element_type=F32).astype(BF16)
        for c in range(3):
            placed[c * half : (c + 1) * half, s * 128 : (s + 1) * 128] = spread[
                :, c * 128 : (c + 1) * 128
            ]
        col_hit = lax.broadcasted_iota(jnp.int32, (tile, 128), 0) == cols_at
        hit[:, s * 128 : (s + 1) * 128] = jnp.where(col_hit, 1.0, 0.0).astype(BF16)
    groups = tile // 128
    for c in range(3):
        for j in range(tile // 256):
            block = lax.dot_general(
                placed[c * half : (c + 1) * half, :], hit[j * 256 : (j + 1) * 256, :], NT,
                preferred_element_type=F32,
            ).astype(BF16)
            for h in range(2):
                start = (c * groups + 2 * j + h) * half
                flat[start : start + half, :] = block[:, h * 128 : (h + 1) * 128]
    part_rows = flat.shape[0] // 2
    forwards = []

    def task(part):
        order = TILE_ORDERS[part]
        base = part * part_rows
        yield from collect(rings, flat, base, part_rows, order, slots, base)
        start, rows = chunk_start(rings, base, part_rows, order)
        here = pl.ds(pl.multiple_of(start, 16), rows)
        tab_ref[rings.core, here, :] = flat[here, :]
        yield from spread_out(rings, tab_ref, base, part_rows, order, forwards)

    run_together(task(part) for part in range(2))
    for block, ticket in forwards:
        rings.arrive(block, ticket)
    rings.finish()


def matrix_call(quads, labels, tile, ring_devices):
    half = tile // 2
    used = 3 * half * (tile // 128)
    unit = 2 * 16 * ring_devices
    rows = -(-used // unit) * unit
    sources = 8
    piece = quads.shape[1]
    return pl.pallas_call(
        matrix_kernel,
        out_shape=jax.ShapeDtypeStruct((2, rows, 128), BF16),
        in_specs=[vmem(), vmem()],
        out_specs=vmem(),
        scratch_shapes=[
            pltpu.VMEM((rows, 128), BF16),
            pltpu.VMEM((rows, 128), BF16),
            pltpu.VMEM((sources, piece, 384), BF16),
            pltpu.VMEM((sources, 8, 128), jnp.int32),
            pltpu.VMEM((3 * half, sources * 128), BF16),
            pltpu.VMEM((tile, sources * 128), BF16),
            pltpu.SemaphoreType.DMA((80,)),
            pltpu.SemaphoreType.DMA((80,)),
        ],
        compiler_params=pltpu.CompilerParams(
            vmem_limit_bytes=VMEM_LIMIT, collective_id=1, has_side_effects=True
        ),
        cost_estimate=pl.CostEstimate(flops=2_000_000_000, bytes_accessed=60_000_000, transcendentals=0),
        name="matrix",
    )(quads, labels)


def layout_kernel(tab_ref, out_ref):
    tile = out_ref.shape[2]
    half = tile // 2
    for h in range(2):
        for g in range(tile // 128):
            out_ref[0, h * half : (h + 1) * half, g * 128 : (g + 1) * 128] = tab_ref[
                h, g * half : (g + 1) * half, :
            ]


def layout_call(tab, tile):
    rows = tile // 2 * (tile // 128)
    return pl.pallas_call(
        layout_kernel,
        grid=(3,),
        out_shape=jax.ShapeDtypeStruct((3, tile, tile), BF16),
        in_specs=[pl.BlockSpec((2, rows, 128), lambda c: (0, c, 0))],
        out_specs=pl.BlockSpec((1, tile, tile), lambda c: (c, 0, 0)),
        compiler_params=pltpu.CompilerParams(vmem_limit_bytes=VMEM_LIMIT),
        name="layout",
    )(tab)


def on_device(
    basis_values,
    density_matrix,
    points,
    weights,
    intersection,
    basis_index,
    atom_positions,
    shell_blocks,
    shell_widths,
    green,
):
    phi, dens, pts = basis_values[0], density_matrix[0], points[0]
    nz, nx = lax.axis_size("batch_0"), lax.axis_size("batch_1")
    n_row, n_col = lax.axis_size("row"), lax.axis_size("col")
    planes = n_row * n_col
    core = lax.axis_index("batch_2")
    plane = lax.axis_index("col") * n_row + lax.axis_index("row")
    held = nz * nx * planes
    count = intersection.shape[1]
    atoms_col = intersection.reshape(count, 1)
    widths = jnp.broadcast_to(shell_widths.reshape(HALF_S, 2).T.reshape(S, 1), (S, 128))

    sibling_atoms = lax.ppermute(intersection, "batch_2", [(0, 1), (1, 0)])
    slot = jnp.arange(held)
    slot_atom = (slot // planes * 2 + core) * planes + slot % planes

    def found(atoms):
        match = slot_atom[None, :] == atoms.reshape(count, 1)
        return (count + jnp.sum(jnp.where(match, jnp.arange(count)[:, None] - count, 0), axis=0))[None]

    own, sib = found(intersection), found(sibling_atoms)
    mine = lax.dynamic_slice_in_dim(green, plane, 1, 0).reshape(DEG, HALF_S, 2, HALF_S, 2)
    mine = mine.transpose(2, 0, 1, 4, 3).reshape(2 * DEG * HALF_S, S)
    labels = jnp.pad(
        basis_index.reshape(2, -1), ((0, 6), (0, 128 - basis_index.shape[1] // 2)),
        constant_values=-(1 << 20),
    )
    atoms = intersection[0]
    spots = {"z": atoms // (nx * 2 * planes), "x": atoms // (2 * planes) % nx, "y": atoms % planes}
    sizes = {"z": nz, "x": nx, "y": planes}
    starts = []
    for part, order in enumerate(ATOM_ORDERS):
        index = 0
        for axis in order:
            index = index * sizes[axis] + spots[axis]
        starts.append(((atoms // planes % 2 * 3 + part) * held + index) * HALF_S)
    starts = jnp.stack(starts)

    moments = moments_call(
        intersection, shell_blocks, atoms_col, atom_positions, pts, weights, widths, phi, dens
    )
    tab, potential = atoms_call(own, sib, moments, mine, planes)
    quads = field_call(
        starts, intersection, shell_blocks, atoms_col, atom_positions, pts, weights, widths, phi,
        tab.reshape(-1, 128),
    )
    tile = NB // n_row
    matrix = matrix_call(quads, labels, tile, nz * nx)
    return potential.reshape(planes, -1), layout_call(matrix, tile)


def solution(mesh):
    split = (8, 4, 2) if mesh.shape["batch"] == 64 else (mesh.shape["batch"] // 4, 2, 2)
    finer = Mesh(
        mesh.devices.reshape(*split, mesh.shape["row"], mesh.shape["col"]),
        BATCH_ROW_COL,
    )
    placed = (
        P(BATCH_ROW_COL, None, None),
        P(BATCH_ROW_COL, None, None, None),
        P(BATCH_ROW_COL, None, None),
        P(BATCH_ROW_COL, None),
        P(BATCH_ROW_COL, None),
        P(BATCH_ROW_COL, None),
        P(),
        P(),
        P(),
        P(BATCH, None, None),
    )
    return jax.shard_map(
        on_device,
        mesh=finer,
        in_specs=placed,
        out_specs=(P(BATCH, None), P(None, "row", "col")),
        check_vma=False,
    )
```

time: 521 us -> 221 us (0.42); the launches traced: 514 us -> 220 us
  waiting for transfers between devices: 308 us -> 0.01 us
  Pallas kernels: 0 us -> 203 us
  matrix products: 54.6 us -> 0 us
  local copies, waits for them, and re-layouts: 60.8 us -> 9.82 us
  starting transfers between devices: 43.1 us -> 3.33 us
  other arithmetic: 22.2 us -> 3.26 us
  between operations: 15.3 us -> 0.71 us
  blocking collectives: 10.1 us -> 0 us
    pallas_call x0 -> x5, Pallas kernels: none -> 203 us  [the longest x1 88.4 us: atoms_call(): pl.pallas_call(atoms_kernel, out_shape=(jax.ShapeDtypeStruct((2, 3 * held...]
    all_to_all x6 -> x0, waiting for transfers between devices: 123 us -> none  [the longest x1 70.6 us: on_device(): lax.all_to_all(outgoing, BATCH, split_axis=0, concat_axis=0, tiled=True)]
    reduce_scatter x2 -> x0, waiting for transfers between devices: 105 us -> none  [scatter_axes(): nearer = lax.psum_scatter(x, axes[0], scatter_dimension=dim, tiled=True)]
    all_gather x2 -> x0, waiting for transfers between devices: 62.7 us -> none  [gather_in_order(): parts = lax.all_gather(parts, axes[k], axis=0, tiled=True)]
    dot_general x20 -> x0, matrix products: 54.6 us -> none  [the longest x4 24.1 us: on_device(): jnp.einsum('ctj,uj->ctu', placed, cols_hit, preferred_element_type=jnp.fl...]
    all_to_all x6 -> x0, starting transfers between devices: 42.6 us -> none  [the longest x1 13.2 us: on_device(): lax.all_to_all(tags, BATCH, split_axis=0, concat_axis=0, tiled=True)]
    unnamed x6 -> x0, waiting for transfers between devices: 17.3 us -> none
    reshape x6 -> x5, local copies, waits for them, and re-layouts: 19.1 us -> 3.75 us  [the longest x2 1.58 us: on_device(): mine = mine.transpose(2, 0, 1, 4, 3).reshape(2 * DEG * HALF_S, S)]
  transfers between devices with their start and end apart: 11 -> 1, of which waited for: 9 -> 0; matrix products, arithmetic and copies ran while one was open for 14% -> 5% of each run, Pallas kernels for 0% -> 9%
where the time goes in v1:
time: 221 us; the launch traced here: 220 us
  Pallas kernels  203 us (92%)
  local copies, waits for them, and re-layouts  9.82 us (4%)
  starting transfers between devices  3.33 us (2%)
  other arithmetic  3.26 us (1%)
    pallas_call x1, Pallas kernels, atoms_call(): pl.pallas_call(atoms_kernel, out_shape=(jax.ShapeDtypeStruct((2, 3 * held...  88.4 us
    pallas_call x1, Pallas kernels, matrix_call(): pl.pallas_call(matrix_kernel, out_shape=jax.ShapeDtypeStruct((2, rows, 12...  74.1 us
    pallas_call x1, Pallas kernels, moments_call(): pl.pallas_call(moments_kernel, out_shape=jax.ShapeDtypeStruct((count + 1,...  20.3 us
    pallas_call x1, Pallas kernels, field_call(): pl.pallas_call(field_kernel, out_shape=jax.ShapeDtypeStruct((4, basis //...  15.6 us
    pallas_call x1, Pallas kernels, layout_call(): pl.pallas_call(layout_kernel, grid=(3,), out_shape=jax.ShapeDtypeStruct((...  4.88 us
  transfers between devices with their start and end apart: 1, of which 0 were waited for; matrix products, arithmetic and copies ran while one was open for 5% of the time, Pallas kernels for 9%

profile of v1, /device:TPU:1, one launch (start us, length us, event | category | flops | bytes accessed | tf_op | source)
XLA Modules:
  0.0 220.4 jit_solution(6475327408534232841)
XLA Ops:
  0.6 0.0 copy-start
  0.6 3.3 %collective-permute-start = (s32[1,32]{1,0:T(1,128)}, s32[1,32]{1,0:T(1,128)S(1)}, u32[]{:S(2)}, u32[]{:S(2)}) collective-permute-start(s32[1,32]{1,0:T(1,128)} %atoms_s.3), channel_id=1, source_target_pairs={{0,4},{4,0},{1,5},{5,1},{2,6},{6,2},{3,7},{7,3},{8,12},{12,8},{9,1... | collective-permute-start | bytes 392 | tf_op jit(solution)/shard_map/ppermute | solution.py:659
  4.0 0.7 add_multiply_fusion.2
  4.7 1.3 copy.22.atoms_ref
  6.0 1.3 copy.34
  7.4 0.7 reshape.81
  8.1 0.1 copy.21
  8.2 0.1 broadcast_in_dim.38
  8.3 0.0 copy-done
  8.3 0.5 copy.23
  8.8 0.8 copy.27
  9.6 0.8 reshape.87.green_ref
  10.4 0.5 broadcast.282
  10.9 1.3 reduce.3
  12.2 0.1 reshape.86
  12.3 0.6 pad_add_fusion.rows_s
  12.9 0.7 broadcast_in_dim.39.widths_ref
  13.6 0.0 copy-start.1
  13.6 20.3 %moments.1.mom_ref = bf16[33,96,128]{2,1,0:T(8,128)(2,1)} custom-call(s32[1,32]{1,0:T(1,128)} %atoms_s.3, s32[256]{0:T(256)} %blocks_s.3, s32[32,1]{1,0:T(8,128)} %copy.22.atoms_ref, f32[3,256]{1,0:T(4,128)} %pos_ref.3, f32[3,2048]{1,0:T(4,128)} %bitcast.25, f32[1,2048]{1,0:T(1,128)} %w_ref.3, f32[64,128]{1,0:T(8,128)} %broadcast_in_dim.39.widths_ref, ...), custom_call_target="tpu_custom_call" | custom-call | flops 4000000000 | bytes 3000000 | tf_op jit(solution)/shard_map/moments/pallas_call | solution.py:122
  33.8 0.6 pad.4.label_ref
  34.4 0.0 collective-permute-done
  34.4 0.0 copy-done.1
  34.4 0.1 select_reduce_fusion
  34.5 0.5 add_bitcast_fusion
  35.1 88.4 %atoms.1 = (bf16[2,12288,128]{2,1,0:T(8,128)(2,1)}, bf16[4,96,128]{2,1,0:T(8,128)(2,1)}) custom-call(s32[1,128]{1,0:T(1,128)} %get-tuple-element.16.own_s, s32[1,128]{1,0:T(1,128)} %get-tuple-element.15.sib_s, bf16[33,96,128]{2,1,0:T(8,128)(2,1)} %moments.1.mom_ref, bf16[512,64]{1,0:T(8,128)(2,1)} %reshape.87.green_ref), custom_call_target="tpu_custom_call" | custom-call | flops 100000000 | bytes 60000000 | tf_op jit(solution)/shard_map/atoms/pallas_call | solution.py:399
  123.5 1.6 copy.33
  125.1 0.7 broadcast_in_dim.40.widths_ref
  125.8 15.6 %field.1.quads_ref = bf16[4,96,384]{2,1,0:T(8,128)(2,1)} custom-call(s32[3,32]{1,0:T(4,128)} %pad_add_fusion.rows_s, s32[1,32]{1,0:T(1,128)} %atoms_s.3, s32[256]{0:T(256)} %blocks_s.3, s32[32,1]{1,0:T(8,128)} %copy.22.atoms_ref, f32[3,256]{1,0:T(4,128)} %pos_ref.3, f32[3,2048]{1,0:T(4,128)} %bitcast.26, f32[1,2048]{1,0:T(1,128)} %w_ref.3, ...), custom_call_target="tpu_custom_call" | custom-call | flops 4000000000 | bytes 8000000 | tf_op jit(solution)/shard_map/field/pallas_call | solution.py:482
  141.4 74.1 %matrix.1.tab_ref = bf16[2,7168,128]{2,1,0:T(8,128)(2,1)} custom-call(bf16[4,96,384]{2,1,0:T(8,128)(2,1)} %field.1.quads_ref, s32[8,128]{1,0:T(8,128)} %pad.4.label_ref), custom_call_target="tpu_custom_call" | custom-call | flops 2000000000 | bytes 60000000 | tf_op jit(solution)/shard_map/matrix/pallas_call | solution.py:590
  215.5 4.9 %layout.1 = bf16[3,768,768]{2,1,0:T(8,128)(2,1)} custom-call(bf16[2,7168,128]{2,1,0:T(8,128)(2,1)} %matrix.1.tab_ref), custom_call_target="tpu_custom_call" | custom-call | tf_op jit(solution)/shard_map/layout/pallas_call | solution.py:625
  (4 shorter events, 0.0 us)
Async XLA Ops:
  0.6 7.6 %copy-start = (bf16[4,8,4096]{2,1,0:T(8,128)(2,1)S(1)}, bf16[4,8,4096]{2,1,0:T(8,128)(2,1)}, u32[]{:S(2)}) copy-start(bf16[4,8,4096]{2,1,0:T(8,128)(2,1)} %param.19) | copy-start | bytes 786436
  0.6 33.8 %collective-permute-start = (s32[1,32]{1,0:T(1,128)}, s32[1,32]{1,0:T(1,128)S(1)}, u32[]{:S(2)}, u32[]{:S(2)}) collective-permute-start(s32[1,32]{1,0:T(1,128)} %atoms_s.3), channel_id=1, source_target_pairs={{0,4},{4,0},{1,5},{5,1},{2,6},{6,2},{3,7},{7,3},{8,12},{12,8},{9,1... | collective-permute-start | bytes 392 | tf_op jit(solution)/shard_map/ppermute | solution.py:659
  13.6 20.9 %copy-start.1 = (s32[1,32]{1,0:T(1,128)S(1)}, s32[1,32]{1,0:T(1,128)}, u32[]{:S(2)}) copy-start(s32[1,32]{1,0:T(1,128)} %atoms_s.3) | copy-start | bytes 388

commit v2 on v1

--- a/solution.py
+++ b/solution.py
@@ -18,6 +18,10 @@
 F32 = jnp.float32
 BF16 = jnp.bfloat16
 HALF_S = S // 2
+RATE = {"z": 90e3, "x": 90e3, "y": 90e3, "core": 250e3}
+HOP = 1.0
+ISSUE = 0.05
+DIRECT = ""
 VMEM_LIMIT = 56 * 1024 * 1024
 NT = (((1,), (1,)), ((), ()))
 
@@ -30,10 +34,17 @@
     return pl.BlockSpec(memory_space=pltpu.SMEM)
 
 
+def as_column(row):
+    count = row.shape[1]
+    down = lax.broadcasted_iota(jnp.int32, (count, count), 0)
+    across = lax.broadcasted_iota(jnp.int32, (count, count), 1)
+    return jnp.sum(jnp.where(down == across, row, 0), axis=1, keepdims=True)
+
+
 def fill_rows(atoms_ref, pos_ref, pts_ref, dist_ref, polar_ref, side_ref):
-    count = atoms_ref.shape[0]
+    count = atoms_ref.shape[1]
     every = pos_ref.shape[1]
-    picked = lax.broadcasted_iota(jnp.int32, (count, every), 1) == atoms_ref[...]
+    picked = lax.broadcasted_iota(jnp.int32, (count, every), 1) == as_column(atoms_ref[...])
     centre = [
         jnp.sum(jnp.where(picked, pos_ref[d : d + 1, :], 0.0), axis=1, keepdims=True)
         for d in range(3)
@@ -57,8 +68,12 @@
     row = lax.broadcasted_iota(jnp.int32, (S, lanes), 0)
     shell = jnp.where(row < HALF_S, 2 * row, 2 * (row - HALF_S) + 1)
     middle = shell.astype(F32) * (4.0 / S)
-    scale = math.sqrt(math.log2(math.e)) / widths_ref[...]
-    return shell, middle, scale
+    row = lax.broadcasted_iota(jnp.int32, (S, S), 0)
+    order = jnp.where(row < HALF_S, 2 * row, 2 * (row - HALF_S) + 1)
+    picked = lax.broadcasted_iota(jnp.int32, (S, S), 1) == order
+    widths = jnp.sum(jnp.where(picked, widths_ref[...], 0.0), axis=1, keepdims=True)
+    scale = math.sqrt(math.log2(math.e)) / widths
+    return shell, middle, jnp.broadcast_to(scale, (S, lanes))
 
 
 def radial_of(dist, middle, scale, live):
@@ -75,9 +90,17 @@
 
 def moments_kernel(
     atoms_s, blocks_s, atoms_ref, pos_ref, pts_ref, w_ref, widths_ref, phi_ref, dens_ref,
-    out_ref, dist_ref, polar_ref, side_ref, wd_ref, scaled_ref, ang_ref, mid_ref, inv_ref,
+    out_ref, own_ref, dist_ref, polar_ref, side_ref, wd_ref, scaled_ref, ang_ref, mid_ref, inv_ref,
 ):
-    count = atoms_ref.shape[0]
+    count = atoms_ref.shape[1]
+    held = own_ref.shape[1]
+    planes = lax.axis_size("row") * lax.axis_size("col")
+    slot = lax.broadcasted_iota(jnp.int32, (count, held), 1)
+    wanted = (slot // planes * 2 + lax.axis_index("batch_2")) * planes + lax.rem(slot, planes)
+    turn = lax.broadcasted_iota(jnp.int32, (count, held), 0)
+    own_ref[...] = count + jnp.sum(
+        jnp.where(as_column(atoms_ref[...]) == wanted, turn - count, 0), axis=0, keepdims=True
+    )
     points = phi_ref.shape[1]
     fill_rows(atoms_ref, pos_ref, pts_ref, dist_ref, polar_ref, side_ref)
     wide = min(512, points)
@@ -121,9 +144,12 @@
     points = phi.shape[1]
     return pl.pallas_call(
         moments_kernel,
-        out_shape=jax.ShapeDtypeStruct((count + 1, 96, 128), BF16),
+        out_shape=(
+            jax.ShapeDtypeStruct((count + 1, 96, 128), BF16),
+            jax.ShapeDtypeStruct((1, pos.shape[1] // 2), jnp.int32),
+        ),
         in_specs=[smem(), smem()] + [vmem()] * 7,
-        out_specs=vmem(),
+        out_specs=(vmem(), vmem()),
         scratch_shapes=[
             pltpu.VMEM((count // 8, 8, points), F32),
             pltpu.VMEM((DEG, count // 8, 8, points), F32),
@@ -145,6 +171,10 @@
         self.send, self.recv = send, recv
         self.used = 0
         self.started = []
+        self.now = 0.0
+        self.free = {}
+        self.lands = {}
+        self.tasks = []
         self.core = lax.axis_index("batch_2")
         self.turn = 1 - 2 * self.core
         rows = lax.axis_size("row")
@@ -179,12 +209,11 @@
         barrier = pltpu.get_barrier_semaphore()
         greeted = 0
         for axis in axes:
-            if self.size[axis] > 1:
-                for shift in (1, -1):
-                    pl.semaphore_signal(
-                        barrier, inc=1, device_id=self.device(axis, shift), device_id_type=MESH
-                    )
-                    greeted += 1
+            for shift in range(1, self.size[axis]):
+                pl.semaphore_signal(
+                    barrier, inc=1, device_id=self.device(axis, shift), device_id_type=MESH
+                )
+                greeted += 1
         for other in others:
             pl.semaphore_signal(barrier, inc=1, device_id=other, device_id_type=MESH)
             greeted += 1
@@ -194,13 +223,41 @@
         self.used += 1
         return self.used - 1
 
-    def copy(self, src, dst, ticket, device):
+    def copy(self, src, dst, ticket, device, link="core", hops=1):
         made = pltpu.make_async_remote_copy(
             src_ref=src, dst_ref=dst, send_sem=self.send.at[ticket],
             recv_sem=self.recv.at[ticket], device_id=device, device_id_type=MESH,
         )
         made.start()
         self.started.append(made)
+        took = hops * math.prod(src.shape) * 2 / RATE[link]
+        self.free[link] = max(self.free.get(link, 0.0), self.now) + took
+        self.lands[ticket] = self.free[link] + HOP
+        self.now += ISSUE
+
+    def spawn(self, work):
+        task = [work, None]
+        self.tasks.append(task)
+        self.step(task)
+        return task
+
+    def step(self, task):
+        try:
+            task[1] = next(task[0])
+        except StopIteration:
+            self.tasks.remove(task)
+
+    def ready(self, task):
+        wanted = task[1]
+        if isinstance(wanted, list):
+            return math.inf if any(other in self.tasks for other in wanted) else self.now
+        return self.lands.get(wanted, math.inf)
+
+    def run(self):
+        while self.tasks:
+            task = min(self.tasks, key=self.ready)
+            self.now = max(self.now, self.ready(task)) + ISSUE
+            self.step(task)
 
     def arrive(self, dst, ticket):
         pltpu.make_async_remote_copy(
@@ -227,36 +284,82 @@
         def own(shift):
             return pl.ds(pl.multiple_of(base + self.place(axis, shift) * rows, 16), rows)
 
-        for t in range(n // 2):
-            for lane, (way, steps) in enumerate(lanes):
-                if t >= steps:
-                    continue
+        def chain(lane, way, steps):
+            for t in range(steps):
                 mine = own(-way * self.turn * (steps - t))
                 if t == 0:
                     source = buf.at[mine]
                 else:
                     source = slots.at[pl.ds(places[lane][t - 1], rows)]
-                    yield
+                    yield tickets[lane][t - 1]
                     self.arrive(source, tickets[lane][t - 1])
                     source[...] = (source[...].astype(F32) + buf[mine, :].astype(F32)).astype(BF16)
                 self.copy(
                     source, slots.at[pl.ds(places[lane][t], rows)], tickets[lane][t],
-                    self.device(axis, -way * self.turn),
+                    self.device(axis, -way * self.turn), axis,
                 )
+
+        for lane, (way, steps) in enumerate(lanes):
+            if steps:
+                self.spawn(chain(lane, way, steps))
         total = buf[own(0), :].astype(F32)
         for lane, (way, steps) in enumerate(lanes):
             if steps:
                 source = slots.at[pl.ds(places[lane][-1], rows)]
-                yield
+                yield tickets[lane][-1]
                 self.arrive(source, tickets[lane][-1])
                 total = total + source[...].astype(F32)
         buf[own(0), :] = total.astype(BF16)
 
+    def far_first(self, axis):
+        return sorted(range(1, self.size[axis]), key=lambda k: -min(k, self.size[axis] - k))
+
+    def reduce_direct(self, buf, base, rows, axis, slots, spot):
+        waits = []
+        for k in self.far_first(axis):
+            ticket = self.ticket()
+            start = pl.multiple_of(base + self.place(axis, k * self.turn) * rows, 16)
+            slot = slots.at[pl.ds(spot + (k - 1) * rows, rows)]
+            hops = min(k, self.size[axis] - k)
+            self.copy(
+                buf.at[pl.ds(start, rows)], slot, ticket,
+                self.device(axis, k * self.turn), axis, hops,
+            )
+            waits.append((ticket, slot))
+        here = pl.ds(pl.multiple_of(base + self.at[axis] * rows, 16), rows)
+        total = buf[here, :].astype(F32)
+        for ticket, slot in waits:
+            yield ticket
+            self.arrive(slot, ticket)
+            total = total + slot[...].astype(F32)
+        buf[here, :] = total.astype(BF16)
+
+    def gather_direct(self, buf, base, rows, axis, arrived=None):
+        def chunk(shift):
+            start = pl.multiple_of(base + self.place(axis, shift * self.turn) * rows, 16)
+            return buf.at[pl.ds(start, rows)]
+
+        waits = []
+        for k in self.far_first(axis):
+            ticket = self.ticket()
+            hops = min(k, self.size[axis] - k)
+            self.copy(
+                chunk(0), chunk(0), ticket, self.device(axis, k * self.turn), axis, hops
+            )
+            waits.append((ticket, k))
+        if arrived:
+            arrived(0)
+        for ticket, k in waits:
+            yield ticket
+            self.arrive(chunk(-k), ticket)
+            if arrived:
+                arrived(-k)
+
     def gather(self, buf, base, rows, axis, arrived=None):
         n = self.size[axis]
-        if arrived:
-            arrived(0)
         if n == 1:
+            if arrived:
+                arrived(0)
             return
         lanes = [(1, n // 2), (-1, n // 2 - 1)]
         tickets = [[self.ticket() for _ in range(steps)] for _, steps in lanes]
@@ -265,28 +368,25 @@
             start = pl.multiple_of(base + self.place(axis, shift) * rows, 16)
             return buf.at[pl.ds(start, rows)]
 
-        for t in range(n // 2 + 1):
-            for lane, (way, steps) in enumerate(lanes):
-                if t > steps or steps == 0:
-                    continue
+        def chain(lane, way, steps):
+            for t in range(steps + 1):
                 block = chunk(way * self.turn * t)
                 if t > 0:
-                    yield
+                    yield tickets[lane][t - 1]
                     self.arrive(block, tickets[lane][t - 1])
                 if t < steps:
-                    self.copy(block, block, tickets[lane][t], self.device(axis, -way * self.turn))
+                    self.copy(
+                        block, block, tickets[lane][t], self.device(axis, -way * self.turn), axis
+                    )
                 if t > 0 and arrived:
                     arrived(way * t)
 
-
-def run_together(tasks):
-    tasks = list(tasks)
-    while tasks:
-        for task in list(tasks):
-            try:
-                next(task)
-            except StopIteration:
-                tasks.remove(task)
+        chains = [
+            self.spawn(chain(lane, way, steps)) for lane, (way, steps) in enumerate(lanes) if steps
+        ]
+        if arrived:
+            arrived(0)
+        yield chains
 
 
 def spread_out(rings, tab, base, total_rows, axes, forwards):
@@ -308,14 +408,16 @@
             rings.copy(tab.at[rings.core, here], tab.at[rings.core, here], ticket, rings.sibling())
             forwards.append((tab.at[1 - rings.core, there], ticket))
 
-        yield from rings.gather(mine, first, rows, axis, forward if depth == 0 else None)
+        step = rings.gather_direct if depth or axis in DIRECT else rings.gather
+        yield from step(mine, first, rows, axis, forward if depth == 0 else None)
 
 
 def collect(rings, buf, base, total_rows, axes, slots, spot):
     rows, start = total_rows, base
-    for axis in axes:
+    for depth, axis in enumerate(axes):
         rows //= rings.size[axis]
-        yield from rings.reduce(buf, start, rows, axis, slots, spot)
+        step = rings.reduce_direct if depth or axis in DIRECT else rings.reduce
+        yield from step(buf, start, rows, axis, slots, spot)
         spot += rows * (rings.size[axis] - 1)
         start = start + rings.at[axis] * rows
 
@@ -328,7 +430,7 @@
     return start, rows
 
 
-ATOM_ORDERS = (("y", "x", "z"), ("z", "y", "x"), ("x", "z", "y"))
+ATOM_ORDERS = (("y", "x", "z"), ("z", "y", "x"), ("x", "y", "z"))
 
 
 def atoms_kernel(
@@ -357,7 +459,7 @@
             dense[pl.ds(row, HALF_S), :] = value[part * HALF_S : (part + 1) * HALF_S]
         return carry
 
-    lax.fori_loop(0, held, fill, 0)
+    lax.fori_loop(0, held, fill, 0, unroll=4)
     forwards = []
     green = green_ref[...]
     column = lax.broadcasted_iota(jnp.int32, (DEG, HALF_S, L), 2) // DEG
@@ -379,7 +481,9 @@
         tab_ref[rings.core, here, :] = jnp.concatenate(sides, axis=1).astype(BF16)
         yield from spread_out(rings, tab_ref, base, part_rows, order, forwards)
 
-    run_together(task(part) for part in range(3))
+    for part in range(3):
+        rings.spawn(task(part))
+    rings.run()
     for slot in range(ny):
         for part, order in enumerate(ATOM_ORDERS):
             index = 0
@@ -408,8 +512,8 @@
             pltpu.VMEM((3 * held * HALF_S, 128), BF16),
             pltpu.VMEM((3 * held * HALF_S, 128), BF16),
             pltpu.VMEM(moments.shape, BF16),
-            pltpu.SemaphoreType.DMA((112,)),
-            pltpu.SemaphoreType.DMA((112,)),
+            pltpu.SemaphoreType.DMA((128,)),
+            pltpu.SemaphoreType.DMA((128,)),
         ],
         compiler_params=pltpu.CompilerParams(
             vmem_limit_bytes=VMEM_LIMIT, collective_id=0, has_side_effects=True
@@ -420,13 +524,15 @@
 
 
 def field_kernel(
-    rows_s, atoms_s, blocks_s, atoms_ref, pos_ref, pts_ref, w_ref, widths_ref, phi_ref, tab_ref,
+    atoms_s, blocks_s, atoms_ref, pos_ref, pts_ref, w_ref, widths_ref, phi_ref, tab_ref,
     out_ref, dist_ref, polar_ref, side_ref, acc_ref, operand_ref, pad_ref, mid_ref, inv_ref,
 ):
-    count = atoms_ref.shape[0]
+    count = atoms_ref.shape[1]
     points = phi_ref.shape[1]
     basis = phi_ref.shape[0]
     piece = basis // 2
+    nx, planes = lax.axis_size("batch_1"), lax.axis_size("row") * lax.axis_size("col")
+    sizes = {"z": lax.axis_size("batch_0"), "x": nx, "y": planes}
     fill_rows(atoms_ref, pos_ref, pts_ref, dist_ref, polar_ref, side_ref)
     wide = min(256, points)
     shell, middle, scale = shell_rows(widths_ref, wide)
@@ -437,10 +543,19 @@
     def eight(group, carry):
         for u in range(8):
             k = group * 8 + u
-            live = shell < 8 * blocks_s[atoms_s[0, k]]
-            packed = [
-                tab_ref[pl.ds(pl.multiple_of(rows_s[c, k], 32), HALF_S), :] for c in range(3)
-            ]
+            atom = atoms_s[0, k]
+            live = shell < 8 * blocks_s[atom]
+            spots = {
+                "z": atom // (nx * 2 * planes),
+                "x": lax.rem(atom // (2 * planes), nx),
+                "y": lax.rem(atom, planes),
+            }
+            packed = []
+            for part, order in enumerate(ATOM_ORDERS):
+                index = lax.rem(atom // planes, 2) * 3 + part
+                for axis in order:
+                    index = index * sizes[axis] + spots[axis]
+                packed.append(tab_ref[pl.ds(pl.multiple_of(index * HALF_S, 32), HALF_S), :])
             packed = jnp.concatenate(packed, axis=0)
             table = jnp.concatenate([packed[:, :L], packed[:, L:]], axis=0)
             for first in range(0, points, wide):
@@ -475,14 +590,14 @@
                 out_ref[r * 2 + q, :, c * 128 : (c + 1) * 128] = local[r * piece : (r + 1) * piece]
 
 
-def field_call(rows, atoms, blocks, atoms_col, pos, pts, w, widths, phi, tab):
+def field_call(atoms, blocks, atoms_col, pos, pts, w, widths, phi, tab):
     count = atoms.shape[1]
     basis, points = phi.shape
     wide = min(256, points)
     return pl.pallas_call(
         field_kernel,
         out_shape=jax.ShapeDtypeStruct((4, basis // 2, 384), BF16),
-        in_specs=[smem()] * 3 + [vmem()] * 7,
+        in_specs=[smem()] * 2 + [vmem()] * 7,
         out_specs=vmem(),
         scratch_shapes=[
             pltpu.VMEM((count // 8, 8, points), F32),
@@ -497,7 +612,7 @@
         compiler_params=pltpu.CompilerParams(vmem_limit_bytes=VMEM_LIMIT),
         cost_estimate=pl.CostEstimate(flops=4_000_000_000, bytes_accessed=8_000_000, transcendentals=4_000_000),
         name="field",
-    )(rows, atoms, blocks, atoms_col, pos, pts, w, jnp.broadcast_to(widths[:, :1], (S, wide)), phi, tab)
+    )(atoms, blocks, atoms_col, pos, pts, w, widths, phi, tab)
 
 
 TILE_ORDERS = (("z", "x"), ("x", "z"))
@@ -574,7 +689,9 @@
         tab_ref[rings.core, here, :] = flat[here, :]
         yield from spread_out(rings, tab_ref, base, part_rows, order, forwards)
 
-    run_together(task(part) for part in range(2))
+    for part in range(2):
+        rings.spawn(task(part))
+    rings.run()
     for block, ticket in forwards:
         rings.arrive(block, ticket)
     rings.finish()
@@ -653,8 +770,7 @@
     plane = lax.axis_index("col") * n_row + lax.axis_index("row")
     held = nz * nx * planes
     count = intersection.shape[1]
-    atoms_col = intersection.reshape(count, 1)
-    widths = jnp.broadcast_to(shell_widths.reshape(HALF_S, 2).T.reshape(S, 1), (S, 128))
+    widths = shell_widths.reshape(1, S)
 
     sibling_atoms = lax.ppermute(intersection, "batch_2", [(0, 1), (1, 0)])
     slot = jnp.arange(held)
@@ -664,30 +780,19 @@
         match = slot_atom[None, :] == atoms.reshape(count, 1)
         return (count + jnp.sum(jnp.where(match, jnp.arange(count)[:, None] - count, 0), axis=0))[None]
 
-    own, sib = found(intersection), found(sibling_atoms)
+    sib = found(sibling_atoms)
     mine = lax.dynamic_slice_in_dim(green, plane, 1, 0).reshape(DEG, HALF_S, 2, HALF_S, 2)
     mine = mine.transpose(2, 0, 1, 4, 3).reshape(2 * DEG * HALF_S, S)
     labels = jnp.pad(
         basis_index.reshape(2, -1), ((0, 6), (0, 128 - basis_index.shape[1] // 2)),
         constant_values=-(1 << 20),
     )
-    atoms = intersection[0]
-    spots = {"z": atoms // (nx * 2 * planes), "x": atoms // (2 * planes) % nx, "y": atoms % planes}
-    sizes = {"z": nz, "x": nx, "y": planes}
-    starts = []
-    for part, order in enumerate(ATOM_ORDERS):
-        index = 0
-        for axis in order:
-            index = index * sizes[axis] + spots[axis]
-        starts.append(((atoms // planes % 2 * 3 + part) * held + index) * HALF_S)
-    starts = jnp.stack(starts)
-
-    moments = moments_call(
-        intersection, shell_blocks, atoms_col, atom_positions, pts, weights, widths, phi, dens
+    moments, own = moments_call(
+        intersection, shell_blocks, intersection, atom_positions, pts, weights, widths, phi, dens
     )
     tab, potential = atoms_call(own, sib, moments, mine, planes)
     quads = field_call(
-        starts, intersection, shell_blocks, atoms_col, atom_positions, pts, weights, widths, phi,
+        intersection, shell_blocks, intersection, atom_positions, pts, weights, widths, phi,
         tab.reshape(-1, 128),
     )
     tile = NB // n_row

time: 221 us -> 193 us (0.87)
  Pallas kernels: 203 us -> 181 us
  local copies, waits for them, and re-layouts: 9.82 us -> 5.32 us
    pallas_call x1, Pallas kernels: 88.4 us -> 74.4 us  [atoms_call(): pl.pallas_call(atoms_kernel, out_shape=(jax.ShapeDtypeStruct((2, 3 * held...]
    pallas_call x1, Pallas kernels: 74.1 us -> 65.8 us  [matrix_call(): pl.pallas_call(matrix_kernel, out_shape=jax.ShapeDtypeStruct((2, rows, 12...]
  transfers between devices with their start and end apart: 1 -> 1, of which waited for: 0 -> 0; matrix products, arithmetic and copies ran while one was open for 5% -> 3% of each run, Pallas kernels for 9% -> 11%
where the time goes in v2:
time: 193 us
  Pallas kernels  181 us (94%)
  local copies, waits for them, and re-layouts  5.32 us (3%)
  starting transfers between devices  3.33 us (2%)
  other arithmetic  1.98 us (1%)
    pallas_call x1, Pallas kernels, atoms_call(): pl.pallas_call(atoms_kernel, out_shape=(jax.ShapeDtypeStruct((2, 3 * held...  74.4 us
    pallas_call x1, Pallas kernels, matrix_call(): pl.pallas_call(matrix_kernel, out_shape=jax.ShapeDtypeStruct((2, rows, 12...  65.8 us
    pallas_call x1, Pallas kernels, moments_call(): pl.pallas_call(moments_kernel, out_shape=(jax.ShapeDtypeStruct((count + 1...  20.3 us
    pallas_call x1, Pallas kernels, field_call(): pl.pallas_call(field_kernel, out_shape=jax.ShapeDtypeStruct((4, basis //...  15.8 us
    pallas_call x1, Pallas kernels, layout_call(): pl.pallas_call(layout_kernel, grid=(3,), out_shape=jax.ShapeDtypeStruct((...  4.91 us
  transfers between devices with their start and end apart: 1, of which 0 were waited for; matrix products, arithmetic and copies ran while one was open for 3% of the time, Pallas kernels for 11%

profile of v2, /device:TPU:1, one launch (start us, length us, event | category | flops | bytes accessed | tf_op | source)
XLA Modules:
  0.0 192.6 jit_solution(1871822670892176115)
XLA Ops:
  0.6 0.0 copy-start
  0.6 3.3 %collective-permute-start = (s32[1,32]{1,0:T(1,128)}, s32[1,32]{1,0:T(1,128)S(1)}, u32[]{:S(2)}, u32[]{:S(2)}) collective-permute-start(s32[1,32]{1,0:T(1,128)} %atoms_ref.3), channel_id=1, source_target_pairs={{0,4},{4,0},{1,5},{5,1},{2,6},{6,2},{3,7},{7,3},{8,12},{12,8},{9,1... | collective-permute-start | bytes 392 | tf_op jit(solution)/shard_map/ppermute | solution.py:775
  4.0 0.0 copy-done
  4.0 0.5 copy.15
  4.5 0.8 copy.18
  5.3 0.8 reshape.68.green_ref
  6.1 1.4 copy.25
  7.4 0.5 broadcast.86
  7.9 1.3 reduce.3
  9.3 0.1 reshape.67
  9.4 20.3 %moments.1 = (bf16[33,96,128]{2,1,0:T(8,128)(2,1)}, s32[1,128]{1,0:T(1,128)}) custom-call(s32[1,32]{1,0:T(1,128)} %atoms_ref.3, s32[256]{0:T(256)} %blocks_s.3, s32[1,32]{1,0:T(1,128)} %atoms_ref.3, f32[3,256]{1,0:T(4,128)} %pos_ref.3, f32[3,2048]{1,0:T(4,128)} %bitcast.20, f32[1,2048]{1,0:T(1,128)} %w_ref.3, f32[1,64]{1,0:T(1,128)} %bitcast.27, ...), custom_call_target="tpu_custom_call" | custom-call | flops 4000000000 | bytes 3000000 | tf_op jit(solution)/shard_map/moments/pallas_call | solution.py:145
  29.7 0.6 pad.4.label_ref
  30.3 0.0 collective-permute-done
  30.3 0.1 select_reduce_fusion
  30.4 0.5 add_bitcast_fusion.sib_s
  30.9 74.4 %atoms.1 = (bf16[2,12288,128]{2,1,0:T(8,128)(2,1)}, bf16[4,96,128]{2,1,0:T(8,128)(2,1)}) custom-call(s32[1,128]{1,0:T(1,128)} %get-tuple-element.6.own_s, s32[1,128]{1,0:T(1,128)} %add_bitcast_fusion.sib_s, bf16[33,96,128]{2,1,0:T(8,128)(2,1)} %get-tuple-element.7.mom_ref, bf16[512,64]{1,0:T(8,128)(2,1)} %reshape.68.green_ref), custom_call_target="tpu_custom_call" | custom-call | flops 100000000 | bytes 60000000 | tf_op jit(solution)/shard_map/atoms/pallas_call | solution.py:503
  105.3 15.8 %field.1.quads_ref = bf16[4,96,384]{2,1,0:T(8,128)(2,1)} custom-call(s32[1,32]{1,0:T(1,128)} %atoms_ref.3, s32[256]{0:T(256)} %blocks_s.3, s32[1,32]{1,0:T(1,128)} %atoms_ref.3, f32[3,256]{1,0:T(4,128)} %pos_ref.3, f32[3,2048]{1,0:T(4,128)} %bitcast.21, f32[1,2048]{1,0:T(1,128)} %w_ref.3, f32[1,64]{1,0:T(1,128)} %bitcast.28, bf16[192,2048]{1,0:T(8,128)(2,1)} %bitcast.25, ...), custom_call_target="tpu_custom_call" | custom-call | flops 4000000000 | bytes 8000000 | tf_op jit(solution)/shard_map/field/pallas_call | solution.py:597
  121.1 65.8 %matrix.1.tab_ref = bf16[2,7168,128]{2,1,0:T(8,128)(2,1)} custom-call(bf16[4,96,384]{2,1,0:T(8,128)(2,1)} %field.1.quads_ref, s32[8,128]{1,0:T(8,128)} %pad.4.label_ref), custom_call_target="tpu_custom_call" | custom-call | flops 2000000000 | bytes 60000000 | tf_op jit(solution)/shard_map/matrix/pallas_call | solution.py:707
  187.0 0.0 copy-start.1
  187.0 4.9 %layout.1 = bf16[3,768,768]{2,1,0:T(8,128)(2,1)} custom-call(bf16[2,7168,128]{2,1,0:T(8,128)(2,1)} %matrix.1.tab_ref), custom_call_target="tpu_custom_call" | custom-call | tf_op jit(solution)/shard_map/layout/pallas_call | solution.py:742
  191.9 0.0 copy-done.1
  191.9 0.7 copy.24
  (3 shorter events, 0.0 us)
Async XLA Ops:
  0.6 3.3 %copy-start = (bf16[4,8,4096]{2,1,0:T(8,128)(2,1)S(1)}, bf16[4,8,4096]{2,1,0:T(8,128)(2,1)}, u32[]{:S(2)}) copy-start(bf16[4,8,4096]{2,1,0:T(8,128)(2,1)} %param.19) | copy-start | bytes 786436
  0.6 29.6 %collective-permute-start = (s32[1,32]{1,0:T(1,128)}, s32[1,32]{1,0:T(1,128)S(1)}, u32[]{:S(2)}, u32[]{:S(2)}) collective-permute-start(s32[1,32]{1,0:T(1,128)} %atoms_ref.3), channel_id=1, source_target_pairs={{0,4},{4,0},{1,5},{5,1},{2,6},{6,2},{3,7},{7,3},{8,12},{12,8},{9,1... | collective-permute-start | bytes 392 | tf_op jit(solution)/shard_map/ppermute | solution.py:775
  187.0 4.9 %copy-start.1 = (bf16[4,96,128]{2,1,0:T(8,128)(2,1)S(1)}, bf16[4,96,128]{2,1,0:T(8,128)(2,1)}, u32[]{:S(2)}) copy-start(bf16[4,96,128]{2,1,0:T(8,128)(2,1)} %get-tuple-element.8) | copy-start | bytes 294916

commit v3 on v2

--- a/solution.py
+++ b/solution.py
@@ -88,19 +88,11 @@
     ).astype(BF16)
 
 
-def moments_kernel(
+def moments_stage(
     atoms_s, blocks_s, atoms_ref, pos_ref, pts_ref, w_ref, widths_ref, phi_ref, dens_ref,
-    out_ref, own_ref, dist_ref, polar_ref, side_ref, wd_ref, scaled_ref, ang_ref, mid_ref, inv_ref,
+    out_ref, dist_ref, polar_ref, side_ref, wd_ref, scaled_ref, ang_ref, mid_ref, inv_ref,
 ):
     count = atoms_ref.shape[1]
-    held = own_ref.shape[1]
-    planes = lax.axis_size("row") * lax.axis_size("col")
-    slot = lax.broadcasted_iota(jnp.int32, (count, held), 1)
-    wanted = (slot // planes * 2 + lax.axis_index("batch_2")) * planes + lax.rem(slot, planes)
-    turn = lax.broadcasted_iota(jnp.int32, (count, held), 0)
-    own_ref[...] = count + jnp.sum(
-        jnp.where(as_column(atoms_ref[...]) == wanted, turn - count, 0), axis=0, keepdims=True
-    )
     points = phi_ref.shape[1]
     fill_rows(atoms_ref, pos_ref, pts_ref, dist_ref, polar_ref, side_ref)
     wide = min(512, points)
@@ -111,7 +103,8 @@
             dphi = jnp.dot(dens_ref[c], phi, preferred_element_type=F32)
             total = jnp.sum(phi.astype(F32) * dphi, axis=0, keepdims=True)
             wd_ref[c : c + 1, cols] = total * w_ref[:, cols]
-    shell, middle, scale = shell_rows(widths_ref, 128)
+    shell, middle, scale = shell_rows(widths_ref, mid_ref.shape[1])
+    shell = shell[:, :128]
     mid_ref[...] = middle
     inv_ref[...] = scale
     out_ref[count] = jnp.zeros((3 * HALF_S, 2 * L), BF16)
@@ -123,7 +116,9 @@
             live = shell < 8 * blocks_s[atoms_s[0, k]]
             for first in range(0, points, 128):
                 cols = slice(first, first + 128)
-                rad = radial_of(dist_ref[group, u : u + 1, cols], mid_ref[...], inv_ref[...], live)
+                rad = radial_of(
+                    dist_ref[group, u : u + 1, cols], mid_ref[:, :128], inv_ref[:, :128], live
+                )
                 for c in range(3):
                     part = (rad * wd_ref[c : c + 1, cols]).astype(BF16)
                     for par in range(2):
@@ -137,33 +132,6 @@
         return carry
 
     lax.fori_loop(0, count // 8, eight, 0)
-
-
-def moments_call(atoms, blocks, atoms_col, pos, pts, w, widths, phi, dens):
-    count = atoms.shape[1]
-    points = phi.shape[1]
-    return pl.pallas_call(
-        moments_kernel,
-        out_shape=(
-            jax.ShapeDtypeStruct((count + 1, 96, 128), BF16),
-            jax.ShapeDtypeStruct((1, pos.shape[1] // 2), jnp.int32),
-        ),
-        in_specs=[smem(), smem()] + [vmem()] * 7,
-        out_specs=(vmem(), vmem()),
-        scratch_shapes=[
-            pltpu.VMEM((count // 8, 8, points), F32),
-            pltpu.VMEM((DEG, count // 8, 8, points), F32),
-            pltpu.VMEM((DEG, count // 8, 8, points), F32),
-            pltpu.VMEM((8, points), F32),
-            pltpu.VMEM((2, 192, points), BF16),
-            pltpu.VMEM((2, L, points), BF16),
-            pltpu.VMEM((S, 128), F32),
-            pltpu.VMEM((S, 128), F32),
-        ],
-        compiler_params=pltpu.CompilerParams(vmem_limit_bytes=VMEM_LIMIT),
-        cost_estimate=pl.CostEstimate(flops=4_000_000_000, bytes_accessed=3_000_000, transcendentals=4_000_000),
-        name="moments",
-    )(atoms, blocks, atoms_col, pos, pts, w, widths, phi, dens)
 
 
 class Rings:
@@ -217,7 +185,7 @@
         for other in others:
             pl.semaphore_signal(barrier, inc=1, device_id=other, device_id_type=MESH)
             greeted += 1
-        pl.semaphore_wait(barrier, greeted)
+        return greeted
 
     def ticket(self):
         self.used += 1
@@ -282,7 +250,7 @@
             spot += rows * steps
 
         def own(shift):
-            return pl.ds(pl.multiple_of(base + self.place(axis, shift) * rows, 16), rows)
+            return pl.ds(base + self.place(axis, shift) * rows, rows)
 
         def chain(lane, way, steps):
             for t in range(steps):
@@ -293,7 +261,7 @@
                     source = slots.at[pl.ds(places[lane][t - 1], rows)]
                     yield tickets[lane][t - 1]
                     self.arrive(source, tickets[lane][t - 1])
-                    source[...] = (source[...].astype(F32) + buf[mine, :].astype(F32)).astype(BF16)
+                    source[...] = (source[...].astype(F32) + buf[mine].astype(F32)).astype(BF16)
                 self.copy(
                     source, slots.at[pl.ds(places[lane][t], rows)], tickets[lane][t],
                     self.device(axis, -way * self.turn), axis,
@@ -302,14 +270,14 @@
         for lane, (way, steps) in enumerate(lanes):
             if steps:
                 self.spawn(chain(lane, way, steps))
-        total = buf[own(0), :].astype(F32)
+        total = buf[own(0)].astype(F32)
         for lane, (way, steps) in enumerate(lanes):
             if steps:
                 source = slots.at[pl.ds(places[lane][-1], rows)]
                 yield tickets[lane][-1]
                 self.arrive(source, tickets[lane][-1])
                 total = total + source[...].astype(F32)
-        buf[own(0), :] = total.astype(BF16)
+        buf[own(0)] = total.astype(BF16)
 
     def far_first(self, axis):
         return sorted(range(1, self.size[axis]), key=lambda k: -min(k, self.size[axis] - k))
@@ -318,7 +286,7 @@
         waits = []
         for k in self.far_first(axis):
             ticket = self.ticket()
-            start = pl.multiple_of(base + self.place(axis, k * self.turn) * rows, 16)
+            start = base + self.place(axis, k * self.turn) * rows
             slot = slots.at[pl.ds(spot + (k - 1) * rows, rows)]
             hops = min(k, self.size[axis] - k)
             self.copy(
@@ -326,17 +294,17 @@
                 self.device(axis, k * self.turn), axis, hops,
             )
             waits.append((ticket, slot))
-        here = pl.ds(pl.multiple_of(base + self.at[axis] * rows, 16), rows)
-        total = buf[here, :].astype(F32)
+        here = pl.ds(base + self.at[axis] * rows, rows)
+        total = buf[here].astype(F32)
         for ticket, slot in waits:
             yield ticket
             self.arrive(slot, ticket)
             total = total + slot[...].astype(F32)
-        buf[here, :] = total.astype(BF16)
+        buf[here] = total.astype(BF16)
 
     def gather_direct(self, buf, base, rows, axis, arrived=None):
         def chunk(shift):
-            start = pl.multiple_of(base + self.place(axis, shift * self.turn) * rows, 16)
+            start = base + self.place(axis, shift * self.turn) * rows
             return buf.at[pl.ds(start, rows)]
 
         waits = []
@@ -365,7 +333,7 @@
         tickets = [[self.ticket() for _ in range(steps)] for _, steps in lanes]
 
         def chunk(shift):
-            start = pl.multiple_of(base + self.place(axis, shift) * rows, 16)
+            start = base + self.place(axis, shift) * rows
             return buf.at[pl.ds(start, rows)]
 
         def chain(lane, way, steps):
@@ -403,8 +371,8 @@
         def forward(shift, axis=axis, first=first, rows=rows):
             ticket = rings.ticket()
             signed = shift * rings.turn
-            here = pl.ds(pl.multiple_of(first + rings.place(axis, signed) * rows, 16), rows)
-            there = pl.ds(pl.multiple_of(first + rings.place(axis, -signed) * rows, 16), rows)
+            here = pl.ds(first + rings.place(axis, signed) * rows, rows)
+            there = pl.ds(first + rings.place(axis, -signed) * rows, rows)
             rings.copy(tab.at[rings.core, here], tab.at[rings.core, here], ticket, rings.sibling())
             forwards.append((tab.at[1 - rings.core, there], ticket))
 
@@ -433,17 +401,10 @@
 ATOM_ORDERS = (("y", "x", "z"), ("z", "y", "x"), ("x", "y", "z"))
 
 
-def atoms_kernel(
-    own_s, sib_s, mom_ref, green_ref, tab_ref, pot_ref, dense, slots, other, send, recv
-):
-    rings = Rings(send, recv)
+def atoms_stage(rings, index_s, mom_ref, other, green_ref, tab_ref, pot_ref, dense, slots):
     nz, nx, ny = (rings.size[a] for a in "zxy")
     held = nz * nx * ny
-    part_rows = held * HALF_S
-    rings.greet("zxy", [rings.sibling()])
-    ticket = rings.ticket()
-    rings.copy(mom_ref, other, ticket, rings.sibling())
-    rings.arrive(other, ticket)
+    part_rows = held
 
     def place(slot, order):
         spots = {"z": slot // (nx * ny), "x": lax.rem(slot // ny, nx), "y": lax.rem(slot, ny)}
@@ -453,10 +414,9 @@
         return index
 
     def fill(slot, carry):
-        value = mom_ref[own_s[0, slot]] + other[sib_s[0, slot]]
+        value = mom_ref[index_s[0, slot]] + other[index_s[1, slot]]
         for part, order in enumerate(ATOM_ORDERS):
-            row = pl.multiple_of(part * part_rows + place(slot, order) * HALF_S, 32)
-            dense[pl.ds(row, HALF_S), :] = value[part * HALF_S : (part + 1) * HALF_S]
+            dense[part * part_rows + place(slot, order)] = value[part * HALF_S : (part + 1) * HALF_S]
         return carry
 
     lax.fori_loop(0, held, fill, 0, unroll=4)
@@ -470,15 +430,14 @@
         base = part * part_rows
         yield from collect(rings, dense, base, part_rows, order, slots, base)
         start, rows = chunk_start(rings, base, part_rows, order)
-        here = pl.ds(pl.multiple_of(start, 32), rows)
-        charges = dense[here, :].astype(F32)
+        charges = dense[start].astype(F32)
         stacked = jnp.concatenate([charges[:, :L], charges[:, L:]], axis=0).astype(BF16)
         result = jnp.dot(green, stacked, preferred_element_type=F32)
         sides = []
         for par in range(2):
             block = result[par * DEG * HALF_S : (par + 1) * DEG * HALF_S].reshape(DEG, HALF_S, L)
             sides.append(jnp.sum(jnp.where(column == layer, block, 0.0), axis=0))
-        tab_ref[rings.core, here, :] = jnp.concatenate(sides, axis=1).astype(BF16)
+        tab_ref[rings.core, start] = jnp.concatenate(sides, axis=1).astype(BF16)
         yield from spread_out(rings, tab_ref, base, part_rows, order, forwards)
 
     for part in range(3):
@@ -489,55 +448,26 @@
             index = 0
             for axis in order:
                 index = index * rings.size[axis] + (slot if axis == "y" else rings.at[axis])
-            row = pl.multiple_of(part * part_rows + index * HALF_S, 32)
             pot_ref[slot, part * HALF_S : (part + 1) * HALF_S, :] = tab_ref[
-                rings.core, pl.ds(row, HALF_S), :
+                rings.core, part * part_rows + index
             ]
     for block, ticket in forwards:
         rings.arrive(block, ticket)
-    rings.finish()
-
-
-def atoms_call(own, sib, moments, green, planes):
-    held = own.shape[1]
-    return pl.pallas_call(
-        atoms_kernel,
-        out_shape=(
-            jax.ShapeDtypeStruct((2, 3 * held * HALF_S, 128), BF16),
-            jax.ShapeDtypeStruct((planes, 96, 128), BF16),
-        ),
-        in_specs=[smem(), smem(), vmem(), vmem()],
-        out_specs=(vmem(), vmem()),
-        scratch_shapes=[
-            pltpu.VMEM((3 * held * HALF_S, 128), BF16),
-            pltpu.VMEM((3 * held * HALF_S, 128), BF16),
-            pltpu.VMEM(moments.shape, BF16),
-            pltpu.SemaphoreType.DMA((128,)),
-            pltpu.SemaphoreType.DMA((128,)),
-        ],
-        compiler_params=pltpu.CompilerParams(
-            vmem_limit_bytes=VMEM_LIMIT, collective_id=0, has_side_effects=True
-        ),
-        cost_estimate=pl.CostEstimate(flops=100_000_000, bytes_accessed=60_000_000, transcendentals=0),
-        name="atoms",
-    )(own, sib, moments, green)
-
-
-def field_kernel(
-    atoms_s, blocks_s, atoms_ref, pos_ref, pts_ref, w_ref, widths_ref, phi_ref, tab_ref,
-    out_ref, dist_ref, polar_ref, side_ref, acc_ref, operand_ref, pad_ref, mid_ref, inv_ref,
+
+
+def field_stage(
+    atoms_s, blocks_s, w_ref, phi_ref, tab_ref, out_ref, dist_ref, polar_ref, side_ref,
+    acc_ref, operand_ref, pad_ref, mid_ref, inv_ref,
 ):
-    count = atoms_ref.shape[1]
-    points = phi_ref.shape[1]
-    basis = phi_ref.shape[0]
+    count = dist_ref.shape[0] * 8
+    basis, points = phi_ref.shape
     piece = basis // 2
+    held = tab_ref.shape[1] // 3
     nx, planes = lax.axis_size("batch_1"), lax.axis_size("row") * lax.axis_size("col")
     sizes = {"z": lax.axis_size("batch_0"), "x": nx, "y": planes}
-    fill_rows(atoms_ref, pos_ref, pts_ref, dist_ref, polar_ref, side_ref)
-    wide = min(256, points)
-    shell, middle, scale = shell_rows(widths_ref, wide)
-    mid_ref[...] = middle
-    inv_ref[...] = scale
+    wide = mid_ref.shape[1]
+    row = lax.broadcasted_iota(jnp.int32, (S, wide), 0)
+    shell = jnp.where(row < HALF_S, 2 * row, 2 * (row - HALF_S) + 1)
     acc_ref[...] = jnp.zeros_like(acc_ref)
 
     def eight(group, carry):
@@ -546,16 +476,16 @@
             atom = atoms_s[0, k]
             live = shell < 8 * blocks_s[atom]
             spots = {
-                "z": atom // (nx * 2 * planes),
-                "x": lax.rem(atom // (2 * planes), nx),
+                "z": lax.div(atom, nx * 2 * planes),
+                "x": lax.rem(lax.div(atom, 2 * planes), nx),
                 "y": lax.rem(atom, planes),
             }
             packed = []
             for part, order in enumerate(ATOM_ORDERS):
-                index = lax.rem(atom // planes, 2) * 3 + part
+                index = 0
                 for axis in order:
                     index = index * sizes[axis] + spots[axis]
-                packed.append(tab_ref[pl.ds(pl.multiple_of(index * HALF_S, 32), HALF_S), :])
+                packed.append(tab_ref[lax.rem(lax.div(atom, planes), 2), part * held + index])
             packed = jnp.concatenate(packed, axis=0)
             table = jnp.concatenate([packed[:, :L], packed[:, L:]], axis=0)
             for first in range(0, points, wide):
@@ -590,57 +520,35 @@
                 out_ref[r * 2 + q, :, c * 128 : (c + 1) * 128] = local[r * piece : (r + 1) * piece]
 
 
-def field_call(atoms, blocks, atoms_col, pos, pts, w, widths, phi, tab):
-    count = atoms.shape[1]
-    basis, points = phi.shape
-    wide = min(256, points)
-    return pl.pallas_call(
-        field_kernel,
-        out_shape=jax.ShapeDtypeStruct((4, basis // 2, 384), BF16),
-        in_specs=[smem()] * 2 + [vmem()] * 7,
-        out_specs=vmem(),
-        scratch_shapes=[
-            pltpu.VMEM((count // 8, 8, points), F32),
-            pltpu.VMEM((DEG, count // 8, 8, points), F32),
-            pltpu.VMEM((DEG, count // 8, 8, points), F32),
-            pltpu.VMEM((3, 8, points), F32),
-            pltpu.VMEM((basis, points), BF16),
-            pltpu.VMEM((2, 128, points), BF16),
-            pltpu.VMEM((S, wide), F32),
-            pltpu.VMEM((S, wide), F32),
-        ],
-        compiler_params=pltpu.CompilerParams(vmem_limit_bytes=VMEM_LIMIT),
-        cost_estimate=pl.CostEstimate(flops=4_000_000_000, bytes_accessed=8_000_000, transcendentals=4_000_000),
-        name="field",
-    )(atoms, blocks, atoms_col, pos, pts, w, widths, phi, tab)
-
-
 TILE_ORDERS = (("z", "x"), ("x", "z"))
 
 
-def matrix_kernel(quads_ref, label_ref, tab_ref, flat, slots, got, marks, placed, hit, send, recv):
-    rings = Rings(send, recv)
+def square_peers():
+    n_row, n_col = lax.axis_size("row"), lax.axis_size("col")
+    return [
+        {
+            "batch_2": lax.rem(lax.axis_index("batch_2") + dc, 2),
+            "row": lax.rem(lax.axis_index("row") + dr, n_row),
+            "col": lax.rem(lax.axis_index("col") + dl, n_col),
+        }
+        for dc in range(2)
+        for dr in range(n_row)
+        for dl in range(n_col)
+        if dc or dr or dl
+    ]
+
+
+def matrix_stage(
+    rings, quads_ref, label_ref, out_ref, tab_ref, flat, slots, got, marks, placed, hit
+):
     row, col, core = (lax.axis_index(a) for a in ("row", "col", "batch_2"))
     n_row, n_col = lax.axis_size("row"), lax.axis_size("col")
     piece = quads_ref.shape[1]
     tile = hit.shape[0]
     half = tile // 2
     me = (core * n_row + row) * n_col + col
-    shifts = [
-        (dc, dr, dl) for dc in range(2) for dr in range(n_row) for dl in range(n_col)
-    ][1:]
-
-    def peer(shift):
-        return {
-            "batch_2": lax.rem(core + shift[0], 2),
-            "row": lax.rem(row + shift[1], n_row),
-            "col": lax.rem(col + shift[2], n_col),
-        }
-
-    rings.greet("zx", [peer(shift) for shift in shifts])
     waits = []
-    for shift in shifts:
-        to = peer(shift)
+    for to in square_peers():
         first, second = rings.ticket(), rings.ticket()
         rings.copy(label_ref, marks.at[me], first, to)
         rings.copy(quads_ref.at[to["row"] * 2 + to["col"]], got.at[me], second, to)
@@ -648,8 +556,8 @@
         waits.append((marks.at[source], first, got.at[source], second))
     marks[me] = label_ref[...]
     got[me] = quads_ref[row * 2 + col]
-    padded = flat.shape[0] - 3 * half * (tile // 128)
-    flat[flat.shape[0] - padded :, :] = jnp.zeros((padded, 128), BF16)
+    padded = flat.shape[0] - 3 * half * (tile // 128) // 16
+    flat[flat.shape[0] - padded :] = jnp.zeros((padded, 16, 128), BF16)
     for mark, first, block, second in waits:
         rings.arrive(mark, first)
         rings.arrive(block, second)
@@ -675,8 +583,10 @@
                 preferred_element_type=F32,
             ).astype(BF16)
             for h in range(2):
-                start = (c * groups + 2 * j + h) * half
-                flat[start : start + half, :] = block[:, h * 128 : (h + 1) * 128]
+                start = (c * groups + 2 * j + h) * half // 16
+                flat[start : start + half // 16] = block[:, h * 128 : (h + 1) * 128].reshape(
+                    half // 16, 16, 128
+                )
     part_rows = flat.shape[0] // 2
     forwards = []
 
@@ -685,8 +595,8 @@
         base = part * part_rows
         yield from collect(rings, flat, base, part_rows, order, slots, base)
         start, rows = chunk_start(rings, base, part_rows, order)
-        here = pl.ds(pl.multiple_of(start, 16), rows)
-        tab_ref[rings.core, here, :] = flat[here, :]
+        here = pl.ds(start, rows)
+        tab_ref[rings.core, here] = flat[here]
         yield from spread_out(rings, tab_ref, base, part_rows, order, forwards)
 
     for part in range(2):
@@ -694,60 +604,94 @@
     rings.run()
     for block, ticket in forwards:
         rings.arrive(block, ticket)
+    for h in range(2):
+        for c in range(3):
+            for g in range(groups):
+                start = (c * groups + g) * half // 16
+                out_ref[c, h * half : (h + 1) * half, g * 128 : (g + 1) * 128] = tab_ref[
+                    h, start : start + half // 16
+                ].reshape(half, 128)
+
+
+def whole_kernel(
+    index_s, atoms_s, blocks_s, atoms_ref, pos_ref, pts_ref, w_ref, widths_ref, phi_ref, dens_ref,
+    green_ref, label_ref, pot_ref, out_ref,
+    dist, polar, side, wd, scaled, ang, mid, inv, mom, other,
+    dense, slots, tab, acc, operand, pad, quads, flat, slots_2, tab_2, got, marks, placed, hit,
+    send, recv,
+):
+    rings = Rings(send, recv)
+    met = [peer for peer in square_peers()]
+    greeted = rings.greet("zx", met)
+    moments_stage(
+        atoms_s, blocks_s, atoms_ref, pos_ref, pts_ref, w_ref, widths_ref, phi_ref, dens_ref,
+        mom, dist, polar, side, wd, scaled, ang, mid, inv,
+    )
+    pl.semaphore_wait(pltpu.get_barrier_semaphore(), greeted)
+    ticket = rings.ticket()
+    rings.copy(mom, other, ticket, rings.sibling())
+    rings.arrive(other, ticket)
+    atoms_stage(rings, index_s, mom, other, green_ref, tab, pot_ref, dense, slots)
+    field_stage(
+        atoms_s, blocks_s, w_ref, phi_ref, tab, quads, dist, polar, side, acc, operand, pad, mid, inv
+    )
+    matrix_stage(
+        rings, quads, label_ref, out_ref, tab_2, flat, slots_2, got, marks, placed, hit
+    )
     rings.finish()
 
 
-def matrix_call(quads, labels, tile, ring_devices):
+def whole_call(index, atoms, blocks, pos, pts, w, widths, phi, dens, green, labels, sizes):
+    count = atoms.shape[1]
+    basis, points = phi.shape
+    ring_devices, planes, tile = sizes
+    held = ring_devices * planes
     half = tile // 2
-    used = 3 * half * (tile // 128)
     unit = 2 * 16 * ring_devices
-    rows = -(-used // unit) * unit
-    sources = 8
-    piece = quads.shape[1]
+    rows = -(-(3 * half * (tile // 128)) // unit) * unit
+    sources = 2 * planes
+    wide = min(256, points)
     return pl.pallas_call(
-        matrix_kernel,
-        out_shape=jax.ShapeDtypeStruct((2, rows, 128), BF16),
-        in_specs=[vmem(), vmem()],
-        out_specs=vmem(),
+        whole_kernel,
+        out_shape=(
+            jax.ShapeDtypeStruct((planes, 96, 128), BF16),
+            jax.ShapeDtypeStruct((3, tile, tile), BF16),
+        ),
+        in_specs=[smem()] * 3 + [vmem()] * 9,
+        out_specs=(vmem(), vmem()),
         scratch_shapes=[
-            pltpu.VMEM((rows, 128), BF16),
-            pltpu.VMEM((rows, 128), BF16),
-            pltpu.VMEM((sources, piece, 384), BF16),
+            pltpu.VMEM((count // 8, 8, points), F32),
+            pltpu.VMEM((DEG, count // 8, 8, points), F32),
+            pltpu.VMEM((DEG, count // 8, 8, points), F32),
+            pltpu.VMEM((8, points), F32),
+            pltpu.VMEM((2, 192, points), BF16),
+            pltpu.VMEM((2, L, points), BF16),
+            pltpu.VMEM((S, wide), F32),
+            pltpu.VMEM((S, wide), F32),
+            pltpu.VMEM((count + 1, 96, 128), BF16),
+            pltpu.VMEM((count + 1, 96, 128), BF16),
+            pltpu.VMEM((3 * held, HALF_S, 128), BF16),
+            pltpu.VMEM((3 * held, HALF_S, 128), BF16),
+            pltpu.VMEM((2, 3 * held, HALF_S, 128), BF16),
+            pltpu.VMEM((3, 8, points), F32),
+            pltpu.VMEM((basis, points), BF16),
+            pltpu.VMEM((2, 128, points), BF16),
+            pltpu.VMEM((4, basis // 2, 384), BF16),
+            pltpu.VMEM((rows // 16, 16, 128), BF16),
+            pltpu.VMEM((rows // 16, 16, 128), BF16),
+            pltpu.VMEM((2, rows // 16, 16, 128), BF16),
+            pltpu.VMEM((sources, basis // 2, 384), BF16),
             pltpu.VMEM((sources, 8, 128), jnp.int32),
             pltpu.VMEM((3 * half, sources * 128), BF16),
             pltpu.VMEM((tile, sources * 128), BF16),
-            pltpu.SemaphoreType.DMA((80,)),
-            pltpu.SemaphoreType.DMA((80,)),
+            pltpu.SemaphoreType.DMA((192,)),
+            pltpu.SemaphoreType.DMA((192,)),
         ],
         compiler_params=pltpu.CompilerParams(
-            vmem_limit_bytes=VMEM_LIMIT, collective_id=1, has_side_effects=True
+            vmem_limit_bytes=VMEM_LIMIT, collective_id=0, has_side_effects=True
         ),
-        cost_estimate=pl.CostEstimate(flops=2_000_000_000, bytes_accessed=60_000_000, transcendentals=0),
-        name="matrix",
-    )(quads, labels)
-
-
-def layout_kernel(tab_ref, out_ref):
-    tile = out_ref.shape[2]
-    half = tile // 2
-    for h in range(2):
-        for g in range(tile // 128):
-            out_ref[0, h * half : (h + 1) * half, g * 128 : (g + 1) * 128] = tab_ref[
-                h, g * half : (g + 1) * half, :
-            ]
-
-
-def layout_call(tab, tile):
-    rows = tile // 2 * (tile // 128)
-    return pl.pallas_call(
-        layout_kernel,
-        grid=(3,),
-        out_shape=jax.ShapeDtypeStruct((3, tile, tile), BF16),
-        in_specs=[pl.BlockSpec((2, rows, 128), lambda c: (0, c, 0))],
-        out_specs=pl.BlockSpec((1, tile, tile), lambda c: (c, 0, 0)),
-        compiler_params=pltpu.CompilerParams(vmem_limit_bytes=VMEM_LIMIT),
-        name="layout",
-    )(tab)
+        name="whole",
+    )(index, atoms, blocks, atoms, pos, pts, w, widths, phi, dens, green, labels)
 
 
 def on_device(
@@ -766,38 +710,31 @@
     nz, nx = lax.axis_size("batch_0"), lax.axis_size("batch_1")
     n_row, n_col = lax.axis_size("row"), lax.axis_size("col")
     planes = n_row * n_col
-    core = lax.axis_index("batch_2")
     plane = lax.axis_index("col") * n_row + lax.axis_index("row")
+    widths = shell_widths.reshape(1, S)
+
+    count = intersection.shape[1]
     held = nz * nx * planes
-    count = intersection.shape[1]
-    widths = shell_widths.reshape(1, S)
-
     sibling_atoms = lax.ppermute(intersection, "batch_2", [(0, 1), (1, 0)])
+    both = jnp.concatenate([intersection, sibling_atoms], axis=0)
     slot = jnp.arange(held)
-    slot_atom = (slot // planes * 2 + core) * planes + slot % planes
-
-    def found(atoms):
-        match = slot_atom[None, :] == atoms.reshape(count, 1)
-        return (count + jnp.sum(jnp.where(match, jnp.arange(count)[:, None] - count, 0), axis=0))[None]
-
-    sib = found(sibling_atoms)
+    slot_atom = (slot // planes * 2 + lax.axis_index("batch_2")) * planes + slot % planes
+    match = both[:, :, None] == slot_atom[None, None, :]
+    index = count + jnp.sum(
+        jnp.where(match, jnp.arange(count)[None, :, None] - count, 0), axis=1
+    )
     mine = lax.dynamic_slice_in_dim(green, plane, 1, 0).reshape(DEG, HALF_S, 2, HALF_S, 2)
     mine = mine.transpose(2, 0, 1, 4, 3).reshape(2 * DEG * HALF_S, S)
     labels = jnp.pad(
         basis_index.reshape(2, -1), ((0, 6), (0, 128 - basis_index.shape[1] // 2)),
         constant_values=-(1 << 20),
     )
-    moments, own = moments_call(
-        intersection, shell_blocks, intersection, atom_positions, pts, weights, widths, phi, dens
-    )
-    tab, potential = atoms_call(own, sib, moments, mine, planes)
-    quads = field_call(
-        intersection, shell_blocks, intersection, atom_positions, pts, weights, widths, phi,
-        tab.reshape(-1, 128),
-    )
     tile = NB // n_row
-    matrix = matrix_call(quads, labels, tile, nz * nx)
-    return potential.reshape(planes, -1), layout_call(matrix, tile)
+    potential, matrix = whole_call(
+        index, intersection, shell_blocks, atom_positions, pts, weights, widths, phi, dens, mine, labels,
+        (nz * nx, planes, tile),
+    )
+    return potential.reshape(planes, -1), matrix
 
 
 def solution(mesh):

time: 193 us -> 174 us (0.902)
  Pallas kernels: 181 us -> 157 us
  local copies, waits for them, and re-layouts: 5.32 us -> 10.2 us
    pallas_call x5 -> x1, Pallas kernels: 181 us -> 157 us  [whole_call(): pl.pallas_call(whole_kernel, out_shape=(jax.ShapeDtypeStruct((planes, 96,...]
    unnamed x7 -> x6, local copies, waits for them, and re-layouts: 2.58 us -> 7.49 us
  transfers between devices with their start and end apart: 1 -> 1, of which waited for: 0 -> 0; matrix products, arithmetic and copies ran while one was open for 3% -> 3% of each run, Pallas kernels for 11% -> 0%
where the time goes in v3:
time: 174 us
  Pallas kernels  157 us (90%)
  local copies, waits for them, and re-layouts  10.2 us (6%)
  starting transfers between devices  3.33 us (2%)
  other arithmetic  2.71 us (2%)
    pallas_call x1, Pallas kernels, whole_call(): pl.pallas_call(whole_kernel, out_shape=(jax.ShapeDtypeStruct((planes, 96,...  157 us
    unnamed x6, local copies, waits for them, and re-layouts  7.49 us
  transfers between devices with their start and end apart: 1, of which 0 were waited for; matrix products, arithmetic and copies ran while one was open for 3% of the time, Pallas kernels for 0%

profile of v3, /device:TPU:1, one launch (start us, length us, event | category | flops | bytes accessed | tf_op | source)
XLA Modules:
  0.0 173.6 jit_solution(1292621880946781170)
XLA Ops:
  0.6 0.0 copy-start
  0.6 3.3 %collective-permute-start = (s32[1,32]{1,0:T(1,128)}, s32[1,32]{1,0:T(1,128)S(1)}, u32[]{:S(2)}, u32[]{:S(2)}) collective-permute-start(s32[1,32]{1,0:T(1,128)} %atoms_ref.1), channel_id=1, source_target_pairs={{0,4},{4,0},{1,5},{5,1},{2,6},{6,2},{3,7},{7,3},{8,12},{12,8},{9,1... | collective-permute-start | bytes 392 | tf_op jit(solution)/shard_map/ppermute | solution.py:718
  4.0 0.5 broadcast.78
  4.5 1.3 reduce.3
  5.8 0.1 reshape.52
  5.9 1.4 copy.25
  7.3 0.0 copy-done
  7.3 0.5 copy.15
  7.8 0.8 copy.18
  8.6 0.8 reshape.54.green_ref
  9.4 0.6 pad.4.label_ref
  10.0 0.0 collective-permute-done
  10.0 0.7 pad_add_fusion
  10.6 0.1 select_reduce_fusion
  10.7 0.6 broadcast_add_fusion.index_s
  11.3 156.6 %whole.1 = (bf16[4,96,128]{2,1,0:T(8,128)(2,1)}, bf16[3,768,768]{2,1,0:T(8,128)(2,1)}) custom-call(s32[2,128]{1,0:T(2,128)} %broadcast_add_fusion.index_s, s32[1,32]{1,0:T(1,128)} %atoms_ref.1, s32[256]{0:T(256)} %blocks_s.1, s32[1,32]{1,0:T(1,128)} %atoms_ref.1, f32[3,256]{1,0:T(4,128)} %pos_ref.1, f32[3,2048]{1,0:T(4,128)} %bitcast.16, f32[1,2048]{1,0:T(1,128)} %w_ref.1, ...), custom_call_target="tpu_custom_call" | custom-call | tf_op jit(solution)/shard_map/whole/pallas_call | solution.py:654
  168.0 1.6 copy.24
  169.5 4.0 %copy.27 = bf16[3,768,768]{2,1,0:T(8,128)(2,1)} copy(bf16[3,768,768]{2,1,0:T(8,128)(2,1)} %get-tuple-element.9) | data formatting | bytes 7077888
  (3 shorter events, 0.0 us)
Async XLA Ops:
  0.6 6.7 %copy-start = (bf16[4,8,4096]{2,1,0:T(8,128)(2,1)S(1)}, bf16[4,8,4096]{2,1,0:T(8,128)(2,1)}, u32[]{:S(2)}) copy-start(bf16[4,8,4096]{2,1,0:T(8,128)(2,1)} %param.19) | copy-start | bytes 786436
  0.6 9.3 %collective-permute-start = (s32[1,32]{1,0:T(1,128)}, s32[1,32]{1,0:T(1,128)S(1)}, u32[]{:S(2)}, u32[]{:S(2)}) collective-permute-start(s32[1,32]{1,0:T(1,128)} %atoms_ref.1), channel_id=1, source_target_pairs={{0,4},{4,0},{1,5},{5,1},{2,6},{6,2},{3,7},{7,3},{8,12},{12,8},{9,1... | collective-permute-start | bytes 392 | tf_op jit(solution)/shard_map/ppermute | solution.py:718

commit v4 on v3

--- a/solution.py
+++ b/solution.py
@@ -19,8 +19,8 @@
 BF16 = jnp.bfloat16
 HALF_S = S // 2
 RATE = {"z": 90e3, "x": 90e3, "y": 90e3, "core": 250e3}
-HOP = 1.0
-ISSUE = 0.05
+HOP = 2.4
+ISSUE = 0.08
 DIRECT = ""
 VMEM_LIMIT = 56 * 1024 * 1024
 NT = (((1,), (1,)), ((), ()))
@@ -51,7 +51,7 @@
     ]
     for group in range(count // 8):
         rows = slice(group * 8, group * 8 + 8)
-        dx, dy, dz = [pts_ref[d : d + 1, :] - centre[d][rows] for d in range(3)]
+        dx, dy, dz = [pts_ref[d] - centre[d][rows] for d in range(3)]
         dist = jnp.sqrt(dx * dx + dy * dy + dz * dz + 0.01)
         inverse = 1.0 / dist
         dist_ref[group] = dist
@@ -241,43 +241,48 @@
         n = self.size[axis]
         if n == 1:
             return
-        here = self.at[axis]
         lanes = [(1, n // 2), (-1, n // 2 - 1)]
-        tickets = [[self.ticket() for _ in range(steps)] for _, steps in lanes]
-        places = []
-        for _, steps in lanes:
-            places.append([spot + rows * k for k in range(steps)])
-            spot += rows * steps
-
-        def own(shift):
-            return pl.ds(base + self.place(axis, shift) * rows, rows)
-
-        def chain(lane, way, steps):
+        subs = 2 if rows % 2 == 0 else 1
+        per = rows // subs
+        tickets, places = {}, {}
+        for sub in range(subs):
+            for lane, (_, steps) in enumerate(lanes):
+                tickets[lane, sub] = [self.ticket() for _ in range(steps)]
+                places[lane, sub] = [spot + per * k for k in range(steps)]
+                spot += per * steps
+
+        def own(shift, sub):
+            return pl.ds(base + self.place(axis, shift) * rows + sub * per, per)
+
+        def chain(lane, sub, way, steps):
+            ticket, spots = tickets[lane, sub], places[lane, sub]
             for t in range(steps):
-                mine = own(-way * self.turn * (steps - t))
+                mine = own(-way * self.turn * (steps - t), sub)
                 if t == 0:
                     source = buf.at[mine]
                 else:
-                    source = slots.at[pl.ds(places[lane][t - 1], rows)]
-                    yield tickets[lane][t - 1]
-                    self.arrive(source, tickets[lane][t - 1])
+                    source = slots.at[pl.ds(spots[t - 1], per)]
+                    yield ticket[t - 1]
+                    self.arrive(source, ticket[t - 1])
                     source[...] = (source[...].astype(F32) + buf[mine].astype(F32)).astype(BF16)
                 self.copy(
-                    source, slots.at[pl.ds(places[lane][t], rows)], tickets[lane][t],
+                    source, slots.at[pl.ds(spots[t], per)], ticket[t],
                     self.device(axis, -way * self.turn), axis,
                 )
 
-        for lane, (way, steps) in enumerate(lanes):
-            if steps:
-                self.spawn(chain(lane, way, steps))
-        total = buf[own(0)].astype(F32)
-        for lane, (way, steps) in enumerate(lanes):
-            if steps:
-                source = slots.at[pl.ds(places[lane][-1], rows)]
-                yield tickets[lane][-1]
-                self.arrive(source, tickets[lane][-1])
-                total = total + source[...].astype(F32)
-        buf[own(0)] = total.astype(BF16)
+        for sub in range(subs):
+            for lane, (way, steps) in enumerate(lanes):
+                if steps:
+                    self.spawn(chain(lane, sub, way, steps))
+        for sub in range(subs):
+            total = buf[own(0, sub)].astype(F32)
+            for lane, (way, steps) in enumerate(lanes):
+                if steps:
+                    source = slots.at[pl.ds(places[lane, sub][-1], per)]
+                    yield tickets[lane, sub][-1]
+                    self.arrive(source, tickets[lane, sub][-1])
+                    total = total + source[...].astype(F32)
+            buf[own(0, sub)] = total.astype(BF16)
 
     def far_first(self, axis):
         return sorted(range(1, self.size[axis]), key=lambda k: -min(k, self.size[axis] - k))
@@ -330,27 +335,33 @@
                 arrived(0)
             return
         lanes = [(1, n // 2), (-1, n // 2 - 1)]
-        tickets = [[self.ticket() for _ in range(steps)] for _, steps in lanes]
-
-        def chunk(shift):
-            start = base + self.place(axis, shift) * rows
-            return buf.at[pl.ds(start, rows)]
-
-        def chain(lane, way, steps):
+        subs = 2 if rows % 2 == 0 else 1
+        per = rows // subs
+        tickets = {}
+        for sub in range(subs):
+            for lane, (_, steps) in enumerate(lanes):
+                tickets[lane, sub] = [self.ticket() for _ in range(steps)]
+
+        def chunk(shift, sub):
+            return buf.at[pl.ds(base + self.place(axis, shift) * rows + sub * per, per)]
+
+        def chain(lane, sub, way, steps):
+            ticket = tickets[lane, sub]
             for t in range(steps + 1):
-                block = chunk(way * self.turn * t)
+                block = chunk(way * self.turn * t, sub)
                 if t > 0:
-                    yield tickets[lane][t - 1]
-                    self.arrive(block, tickets[lane][t - 1])
+                    yield ticket[t - 1]
+                    self.arrive(block, ticket[t - 1])
                 if t < steps:
-                    self.copy(
-                        block, block, tickets[lane][t], self.device(axis, -way * self.turn), axis
-                    )
+                    self.copy(block, block, ticket[t], self.device(axis, -way * self.turn), axis)
                 if t > 0 and arrived:
-                    arrived(way * t)
+                    arrived(way * t, sub, subs)
 
         chains = [
-            self.spawn(chain(lane, way, steps)) for lane, (way, steps) in enumerate(lanes) if steps
+            self.spawn(chain(lane, sub, way, steps))
+            for sub in range(subs)
+            for lane, (way, steps) in enumerate(lanes)
+            if steps
         ]
         if arrived:
             arrived(0)
@@ -368,11 +379,12 @@
     for depth in reversed(range(len(levels))):
         axis, first, rows = levels[depth]
 
-        def forward(shift, axis=axis, first=first, rows=rows):
+        def forward(shift, sub=0, subs=1, axis=axis, first=first, rows=rows):
             ticket = rings.ticket()
             signed = shift * rings.turn
-            here = pl.ds(first + rings.place(axis, signed) * rows, rows)
-            there = pl.ds(first + rings.place(axis, -signed) * rows, rows)
+            per = rows // subs
+            here = pl.ds(first + rings.place(axis, signed) * rows + sub * per, per)
+            there = pl.ds(first + rings.place(axis, -signed) * rows + sub * per, per)
             rings.copy(tab.at[rings.core, here], tab.at[rings.core, here], ticket, rings.sibling())
             forwards.append((tab.at[1 - rings.core, there], ticket))
 
@@ -517,7 +529,7 @@
                 operand_ref[...], pad_ref[q], NT, preferred_element_type=F32
             ).astype(BF16)
             for r in range(2):
-                out_ref[r * 2 + q, :, c * 128 : (c + 1) * 128] = local[r * piece : (r + 1) * piece]
+                out_ref[r * 2 + q, c] = local[r * piece : (r + 1) * piece]
 
 
 TILE_ORDERS = (("z", "x"), ("x", "z"))
@@ -543,7 +555,7 @@
 ):
     row, col, core = (lax.axis_index(a) for a in ("row", "col", "batch_2"))
     n_row, n_col = lax.axis_size("row"), lax.axis_size("col")
-    piece = quads_ref.shape[1]
+    piece = quads_ref.shape[2]
     tile = hit.shape[0]
     half = tile // 2
     me = (core * n_row + row) * n_col + col
@@ -551,11 +563,12 @@
     for to in square_peers():
         first, second = rings.ticket(), rings.ticket()
         rings.copy(label_ref, marks.at[me], first, to)
-        rings.copy(quads_ref.at[to["row"] * 2 + to["col"]], got.at[me], second, to)
+        wanted = quads_ref.at[to["row"] * 2 + to["col"], pl.ds(to["batch_2"], 2)]
+        rings.copy(wanted, got.at[me], second, to)
         source = (to["batch_2"] * n_row + to["row"]) * n_col + to["col"]
         waits.append((marks.at[source], first, got.at[source], second))
     marks[me] = label_ref[...]
-    got[me] = quads_ref[row * 2 + col]
+    got[me] = quads_ref[row * 2 + col, pl.ds(core, 2)]
     padded = flat.shape[0] - 3 * half * (tile // 128) // 16
     flat[flat.shape[0] - padded :] = jnp.zeros((padded, 16, 128), BF16)
     for mark, first, block, second in waits:
@@ -564,15 +577,13 @@
     sources = 2 * n_row * n_col
     for s in range(sources):
         label = marks[s]
-        rows_at = jnp.where(row == 0, label[0:1, :], label[1:2, :]) - row * tile - core * half
+        rows_at = jnp.where(row == 0, label[0:1, :], label[1:2, :]) - row * tile
         cols_at = jnp.where(col == 0, label[0:1, :], label[1:2, :]) - col * tile
-        row_hit = lax.broadcasted_iota(jnp.int32, (half, 128), 0) == rows_at
-        row_hit = jnp.where(row_hit, 1.0, 0.0).astype(BF16)[:, :piece]
-        spread = jnp.dot(row_hit, got[s], preferred_element_type=F32).astype(BF16)
-        for c in range(3):
-            placed[c * half : (c + 1) * half, s * 128 : (s + 1) * 128] = spread[
-                :, c * 128 : (c + 1) * 128
-            ]
+        for first, count, shift, which in ((0, tile, 0, core), (tile, half, core * half, 1 - core)):
+            row_hit = lax.broadcasted_iota(jnp.int32, (count, 128), 0) == rows_at - shift
+            row_hit = jnp.where(row_hit, 1.0, 0.0).astype(BF16)[:, :piece]
+            spread = jnp.dot(row_hit, got[s, which], preferred_element_type=F32).astype(BF16)
+            placed[first : first + count, s * 128 : (s + 1) * 128] = spread
         col_hit = lax.broadcasted_iota(jnp.int32, (tile, 128), 0) == cols_at
         hit[:, s * 128 : (s + 1) * 128] = jnp.where(col_hit, 1.0, 0.0).astype(BF16)
     groups = tile // 128
@@ -605,24 +616,30 @@
     for block, ticket in forwards:
         rings.arrive(block, ticket)
     for h in range(2):
-        for c in range(3):
+        for c, (comp, first) in enumerate(((2 * h, 0), (2 * h, half), (1, h * half))):
             for g in range(groups):
                 start = (c * groups + g) * half // 16
-                out_ref[c, h * half : (h + 1) * half, g * 128 : (g + 1) * 128] = tab_ref[
+                out_ref[comp, first : first + half, g * 128 : (g + 1) * 128] = tab_ref[
                     h, start : start + half // 16
                 ].reshape(half, 128)
 
 
 def whole_kernel(
     index_s, atoms_s, blocks_s, atoms_ref, pos_ref, pts_ref, w_ref, widths_ref, phi_ref, dens_ref,
-    green_ref, label_ref, pot_ref, out_ref,
+    green_ref, basis_ref, pot_ref, out_ref,
     dist, polar, side, wd, scaled, ang, mid, inv, mom, other,
     dense, slots, tab, acc, operand, pad, quads, flat, slots_2, tab_2, got, marks, placed, hit,
-    send, recv,
+    label, send, recv,
 ):
     rings = Rings(send, recv)
     met = [peer for peer in square_peers()]
     greeted = rings.greet("zx", met)
+    none = jnp.full((8, 128), -(1 << 20), jnp.int32)
+    label[...] = none
+    piece = basis_ref.shape[1] // 2
+    for q in range(2):
+        part = basis_ref[:, q * piece : (q + 1) * piece]
+        label[q : q + 1, :] = jnp.concatenate([part, none[:1, piece:]], axis=1)
     moments_stage(
         atoms_s, blocks_s, atoms_ref, pos_ref, pts_ref, w_ref, widths_ref, phi_ref, dens_ref,
         mom, dist, polar, side, wd, scaled, ang, mid, inv,
@@ -636,7 +653,7 @@
         atoms_s, blocks_s, w_ref, phi_ref, tab, quads, dist, polar, side, acc, operand, pad, mid, inv
     )
     matrix_stage(
-        rings, quads, label_ref, out_ref, tab_2, flat, slots_2, got, marks, placed, hit
+        rings, quads, label, out_ref, tab_2, flat, slots_2, got, marks, placed, hit
     )
     rings.finish()
 
@@ -676,16 +693,17 @@
             pltpu.VMEM((3, 8, points), F32),
             pltpu.VMEM((basis, points), BF16),
             pltpu.VMEM((2, 128, points), BF16),
-            pltpu.VMEM((4, basis // 2, 384), BF16),
+            pltpu.VMEM((4, 3, basis // 2, 128), BF16),
             pltpu.VMEM((rows // 16, 16, 128), BF16),
             pltpu.VMEM((rows // 16, 16, 128), BF16),
             pltpu.VMEM((2, rows // 16, 16, 128), BF16),
-            pltpu.VMEM((sources, basis // 2, 384), BF16),
+            pltpu.VMEM((sources, 2, basis // 2, 128), BF16),
             pltpu.VMEM((sources, 8, 128), jnp.int32),
             pltpu.VMEM((3 * half, sources * 128), BF16),
             pltpu.VMEM((tile, sources * 128), BF16),
-            pltpu.SemaphoreType.DMA((192,)),
-            pltpu.SemaphoreType.DMA((192,)),
+            pltpu.VMEM((8, 128), jnp.int32),
+            pltpu.SemaphoreType.DMA((256,)),
+            pltpu.SemaphoreType.DMA((256,)),
         ],
         compiler_params=pltpu.CompilerParams(
             vmem_limit_bytes=VMEM_LIMIT, collective_id=0, has_side_effects=True
@@ -706,7 +724,7 @@
     shell_widths,
     green,
 ):
-    phi, dens, pts = basis_values[0], density_matrix[0], points[0]
+    phi, dens, pts = basis_values[0], density_matrix[0], points.transpose(1, 0, 2)
     nz, nx = lax.axis_size("batch_0"), lax.axis_size("batch_1")
     n_row, n_col = lax.axis_size("row"), lax.axis_size("col")
     planes = n_row * n_col
@@ -725,13 +743,9 @@
     )
     mine = lax.dynamic_slice_in_dim(green, plane, 1, 0).reshape(DEG, HALF_S, 2, HALF_S, 2)
     mine = mine.transpose(2, 0, 1, 4, 3).reshape(2 * DEG * HALF_S, S)
-    labels = jnp.pad(
-        basis_index.reshape(2, -1), ((0, 6), (0, 128 - basis_index.shape[1] // 2)),
-        constant_values=-(1 << 20),
-    )
     tile = NB // n_row
     potential, matrix = whole_call(
-        index, intersection, shell_blocks, atom_positions, pts, weights, widths, phi, dens, mine, labels,
+        index, intersection, shell_blocks, atom_positions, pts, weights, widths, phi, dens, mine, basis_index,
         (nz * nx, planes, tile),
     )
     return potential.reshape(planes, -1), matrix

time: 174 us -> 166 us (0.954)
  Pallas kernels: 157 us -> 152 us
  local copies, waits for them, and re-layouts: 10.2 us -> 7.7 us
    pallas_call x1, Pallas kernels: 157 us -> 152 us  [whole_call(): pl.pallas_call(whole_kernel, out_shape=(jax.ShapeDtypeStruct((planes, 96,...]
    unnamed x6 -> x4, local copies, waits for them, and re-layouts: 7.49 us -> 5.61 us
  transfers between devices with their start and end apart: 1 -> 1, of which waited for: 0 -> 0; matrix products, arithmetic and copies ran while one was open for 3% -> 1% of each run, Pallas kernels for 0% -> 0%
where the time goes in v4:
time: 166 us; the launch traced here: 165 us
  Pallas kernels  152 us (92%)
  local copies, waits for them, and re-layouts  7.7 us (5%)
  starting transfers between devices  3.33 us (2%)
    pallas_call x1, Pallas kernels, whole_call(): pl.pallas_call(whole_kernel, out_shape=(jax.ShapeDtypeStruct((planes, 96,...  152 us
    unnamed x4, local copies, waits for them, and re-layouts  5.61 us
    ppermute x1, starting transfers between devices, on_device(): sibling_atoms = lax.ppermute(intersection, 'batch_2', [(0, 1), (1, 0)])  3.33 us
  transfers between devices with their start and end apart: 1, of which 0 were waited for; matrix products, arithmetic and copies ran while one was open for 1% of the time, Pallas kernels for 0%

profile of v4, /device:TPU:1, one launch (start us, length us, event | category | flops | bytes accessed | tf_op | source)
XLA Modules:
  0.0 165.5 jit_solution(10599008548014044523)
XLA Ops:
  0.6 0.0 copy-start
  0.6 3.3 %collective-permute-start = (s32[1,32]{1,0:T(1,128)}, s32[1,32]{1,0:T(1,128)S(1)}, u32[]{:S(2)}, u32[]{:S(2)}) collective-permute-start(s32[1,32]{1,0:T(1,128)} %atoms_ref.1), channel_id=1, source_target_pairs={{0,4},{4,0},{1,5},{5,1},{2,6},{6,2},{3,7},{7,3},{8,12},{12,8},{9,1... | collective-permute-start | bytes 392 | tf_op jit(solution)/shard_map/ppermute | solution.py:736
  4.0 0.0 copy-done
  4.0 0.5 copy.15
  4.5 0.8 copy.18
  5.3 0.8 reshape.50.green_ref
  6.1 0.0 collective-permute-done
  6.1 0.7 pad_add_fusion
  6.8 0.1 select_reduce_fusion
  6.9 0.6 broadcast_add_fusion.index_s
  7.4 152.4 %whole.1 = (bf16[4,96,128]{2,1,0:T(8,128)(2,1)}, bf16[3,768,768]{2,1,0:T(8,128)(2,1)}) custom-call(s32[2,128]{1,0:T(2,128)} %broadcast_add_fusion.index_s, s32[1,32]{1,0:T(1,128)} %atoms_ref.1, s32[256]{0:T(256)} %blocks_s.1, s32[1,32]{1,0:T(1,128)} %atoms_ref.1, f32[3,256]{1,0:T(4,128)} %pos_ref.1, f32[3,1,2048]{2,1,0:T(1,128)} %bitcast.16, ...), custom_call_target="tpu_custom_call" | custom-call | tf_op jit(solution)/shard_map/whole/pallas_call | solution.py:671
  159.9 1.6 copy.22
  161.5 4.0 %copy.24 = bf16[3,768,768]{2,1,0:T(8,128)(2,1)} copy(bf16[3,768,768]{2,1,0:T(8,128)(2,1)} %get-tuple-element.9) | data formatting | bytes 7077888
  (3 shorter events, 0.0 us)
Async XLA Ops:
  0.6 3.4 %copy-start = (bf16[4,8,4096]{2,1,0:T(8,128)(2,1)S(1)}, bf16[4,8,4096]{2,1,0:T(8,128)(2,1)}, u32[]{:S(2)}) copy-start(bf16[4,8,4096]{2,1,0:T(8,128)(2,1)} %param.19) | copy-start | bytes 786436
  0.6 5.4 %collective-permute-start = (s32[1,32]{1,0:T(1,128)}, s32[1,32]{1,0:T(1,128)S(1)}, u32[]{:S(2)}, u32[]{:S(2)}) collective-permute-start(s32[1,32]{1,0:T(1,128)} %atoms_ref.1), channel_id=1, source_target_pairs={{0,4},{4,0},{1,5},{5,1},{2,6},{6,2},{3,7},{7,3},{8,12},{12,8},{9,1... | collective-permute-start | bytes 392 | tf_op jit(solution)/shard_map/ppermute | solution.py:736

commit v5 on v4

--- a/solution.py
+++ b/solution.py
@@ -91,6 +91,7 @@
 def moments_stage(
     atoms_s, blocks_s, atoms_ref, pos_ref, pts_ref, w_ref, widths_ref, phi_ref, dens_ref,
     out_ref, dist_ref, polar_ref, side_ref, wd_ref, scaled_ref, ang_ref, mid_ref, inv_ref,
+    between,
 ):
     count = atoms_ref.shape[1]
     points = phi_ref.shape[1]
@@ -131,7 +132,10 @@
             out_ref[k] = jnp.concatenate([got[:96], got[96:]], axis=1).astype(BF16)
         return carry
 
-    lax.fori_loop(0, count // 8, eight, 0)
+    groups = count // 8
+    lax.fori_loop(0, groups // 2, eight, 0)
+    between()
+    lax.fori_loop(groups // 2, groups, eight, 0)
 
 
 class Rings:
@@ -551,41 +555,41 @@
 
 
 def matrix_stage(
-    rings, quads_ref, label_ref, out_ref, tab_ref, flat, slots, got, marks, placed, hit
+    rings, labels, quads_ref, label_ref, out_ref, tab_ref, flat, slots, got, marks, placed, hit
 ):
     row, col, core = (lax.axis_index(a) for a in ("row", "col", "batch_2"))
     n_row, n_col = lax.axis_size("row"), lax.axis_size("col")
     piece = quads_ref.shape[2]
     tile = hit.shape[0]
     half = tile // 2
-    me = (core * n_row + row) * n_col + col
     waits = []
-    for to in square_peers():
-        first, second = rings.ticket(), rings.ticket()
-        rings.copy(label_ref, marks.at[me], first, to)
+    for j, to in enumerate(square_peers()):
+        waits.append((got.at[j + 1], rings.ticket()))
         wanted = quads_ref.at[to["row"] * 2 + to["col"], pl.ds(to["batch_2"], 2)]
-        rings.copy(wanted, got.at[me], second, to)
-        source = (to["batch_2"] * n_row + to["row"]) * n_col + to["col"]
-        waits.append((marks.at[source], first, got.at[source], second))
-    marks[me] = label_ref[...]
-    got[me] = quads_ref[row * 2 + col, pl.ds(core, 2)]
+        rings.copy(wanted, *waits[j], to)
+    marks[0] = label_ref[...]
+    got[0] = quads_ref[row * 2 + col, pl.ds(core, 2)]
     padded = flat.shape[0] - 3 * half * (tile // 128) // 16
     flat[flat.shape[0] - padded :] = jnp.zeros((padded, 16, 128), BF16)
-    for mark, first, block, second in waits:
-        rings.arrive(mark, first)
-        rings.arrive(block, second)
+    for mark, ticket in labels:
+        rings.arrive(mark, ticket)
     sources = 2 * n_row * n_col
     for s in range(sources):
         label = marks[s]
+        cols_at = jnp.where(col == 0, label[0:1, :], label[1:2, :]) - col * tile
+        col_hit = lax.broadcasted_iota(jnp.int32, (tile, 128), 0) == cols_at
+        hit[:, s * 128 : (s + 1) * 128] = jnp.where(col_hit, 1.0, 0.0).astype(BF16)
+    near = [0] + sorted(range(1, sources), key=lambda s: (s % (n_row * n_col) != 0, s % 4 == 1))
+    for s in near:
+        if s:
+            rings.arrive(*waits[s - 1])
+        label = marks[s]
         rows_at = jnp.where(row == 0, label[0:1, :], label[1:2, :]) - row * tile
-        cols_at = jnp.where(col == 0, label[0:1, :], label[1:2, :]) - col * tile
         for first, count, shift, which in ((0, tile, 0, core), (tile, half, core * half, 1 - core)):
             row_hit = lax.broadcasted_iota(jnp.int32, (count, 128), 0) == rows_at - shift
             row_hit = jnp.where(row_hit, 1.0, 0.0).astype(BF16)[:, :piece]
             spread = jnp.dot(row_hit, got[s, which], preferred_element_type=F32).astype(BF16)
             placed[first : first + count, s * 128 : (s + 1) * 128] = spread
-        col_hit = lax.broadcasted_iota(jnp.int32, (tile, 128), 0) == cols_at
-        hit[:, s * 128 : (s + 1) * 128] = jnp.where(col_hit, 1.0, 0.0).astype(BF16)
     groups = tile // 128
     for c in range(3):
         for j in range(tile // 256):
@@ -629,7 +633,7 @@
     green_ref, basis_ref, pot_ref, out_ref,
     dist, polar, side, wd, scaled, ang, mid, inv, mom, other,
     dense, slots, tab, acc, operand, pad, quads, flat, slots_2, tab_2, got, marks, placed, hit,
-    label, send, recv,
+    label, stage_a, stage_b, send, recv,
 ):
     rings = Rings(send, recv)
     met = [peer for peer in square_peers()]
@@ -640,20 +644,33 @@
     for q in range(2):
         part = basis_ref[:, q * piece : (q + 1) * piece]
         label[q : q + 1, :] = jnp.concatenate([part, none[:1, piece:]], axis=1)
+    early = stage_a.shape[0]
+    labels, halves = [], []
+
+    def send_early():
+        pl.semaphore_wait(pltpu.get_barrier_semaphore(), greeted)
+        stage_a[...] = mom[:early]
+        halves.append((other.at[pl.ds(0, early)], rings.ticket()))
+        rings.copy(stage_a, *halves[0], rings.sibling())
+        for j, to in enumerate(met):
+            labels.append((marks.at[j + 1], rings.ticket()))
+            rings.copy(label, *labels[j], to)
+
     moments_stage(
         atoms_s, blocks_s, atoms_ref, pos_ref, pts_ref, w_ref, widths_ref, phi_ref, dens_ref,
-        mom, dist, polar, side, wd, scaled, ang, mid, inv,
+        mom, dist, polar, side, wd, scaled, ang, mid, inv, send_early,
     )
-    pl.semaphore_wait(pltpu.get_barrier_semaphore(), greeted)
-    ticket = rings.ticket()
-    rings.copy(mom, other, ticket, rings.sibling())
-    rings.arrive(other, ticket)
+    stage_b[...] = mom[early:]
+    halves.append((other.at[pl.ds(early, stage_b.shape[0])], rings.ticket()))
+    rings.copy(stage_b, *halves[1], rings.sibling())
+    for block, ticket in halves:
+        rings.arrive(block, ticket)
     atoms_stage(rings, index_s, mom, other, green_ref, tab, pot_ref, dense, slots)
     field_stage(
         atoms_s, blocks_s, w_ref, phi_ref, tab, quads, dist, polar, side, acc, operand, pad, mid, inv
     )
     matrix_stage(
-        rings, quads, label, out_ref, tab_2, flat, slots_2, got, marks, placed, hit
+        rings, labels, quads, label, out_ref, tab_2, flat, slots_2, got, marks, placed, hit
     )
     rings.finish()
 
@@ -702,6 +719,8 @@
             pltpu.VMEM((3 * half, sources * 128), BF16),
             pltpu.VMEM((tile, sources * 128), BF16),
             pltpu.VMEM((8, 128), jnp.int32),
+            pltpu.VMEM((count // 2, 96, 128), BF16),
+            pltpu.VMEM((count // 2 + 1, 96, 128), BF16),
             pltpu.SemaphoreType.DMA((256,)),
             pltpu.SemaphoreType.DMA((256,)),
         ],

time: 166 us -> 164 us (0.988)
  Pallas kernels: 152 us -> 150 us
    pallas_call x1, Pallas kernels: 152 us -> 150 us  [whole_call(): pl.pallas_call(whole_kernel, out_shape=(jax.ShapeDtypeStruct((planes, 96,...]
where the time goes in v5:
time: 164 us; the launch traced here: 163 us
  Pallas kernels  150 us (91%)
  local copies, waits for them, and re-layouts  7.7 us (5%)
  starting transfers between devices  3.33 us (2%)
    pallas_call x1, Pallas kernels, whole_call(): pl.pallas_call(whole_kernel, out_shape=(jax.ShapeDtypeStruct((planes, 96,...  150 us
    unnamed x4, local copies, waits for them, and re-layouts  5.61 us
    ppermute x1, starting transfers between devices, on_device(): sibling_atoms = lax.ppermute(intersection, 'batch_2', [(0, 1), (1, 0)])  3.33 us
  transfers between devices with their start and end apart: 1, of which 0 were waited for; matrix products, arithmetic and copies ran while one was open for 1% of the time, Pallas kernels for 0%

profile of v5, /device:TPU:1, one launch (start us, length us, event | category | flops | bytes accessed | tf_op | source)
XLA Modules:
  0.0 163.4 jit_solution(8488732936906211198)
XLA Ops:
  0.6 0.0 copy-start
  0.6 3.3 %collective-permute-start = (s32[1,32]{1,0:T(1,128)}, s32[1,32]{1,0:T(1,128)S(1)}, u32[]{:S(2)}, u32[]{:S(2)}) collective-permute-start(s32[1,32]{1,0:T(1,128)} %atoms_ref.1), channel_id=1, source_target_pairs={{0,4},{4,0},{1,5},{5,1},{2,6},{6,2},{3,7},{7,3},{8,12},{12,8},{9,1... | collective-permute-start | bytes 392 | tf_op jit(solution)/shard_map/ppermute | solution.py:755
  4.0 0.0 copy-done
  4.0 0.5 copy.15
  4.5 0.8 copy.18
  5.3 0.8 reshape.50.green_ref
  6.1 0.0 collective-permute-done
  6.1 0.7 pad_add_fusion
  6.8 0.1 select_reduce_fusion
  6.9 0.6 broadcast_add_fusion.index_s
  7.4 150.4 %whole.1 = (bf16[4,96,128]{2,1,0:T(8,128)(2,1)}, bf16[3,768,768]{2,1,0:T(8,128)(2,1)}) custom-call(s32[2,128]{1,0:T(2,128)} %broadcast_add_fusion.index_s, s32[1,32]{1,0:T(1,128)} %atoms_ref.1, s32[256]{0:T(256)} %blocks_s.1, s32[1,32]{1,0:T(1,128)} %atoms_ref.1, f32[3,256]{1,0:T(4,128)} %pos_ref.1, f32[3,1,2048]{2,1,0:T(1,128)} %bitcast.16, ...), custom_call_target="tpu_custom_call" | custom-call | tf_op jit(solution)/shard_map/whole/pallas_call | solution.py:688
  157.8 1.6 copy.22
  159.4 4.0 %copy.24 = bf16[3,768,768]{2,1,0:T(8,128)(2,1)} copy(bf16[3,768,768]{2,1,0:T(8,128)(2,1)} %get-tuple-element.9) | data formatting | bytes 7077888
  (3 shorter events, 0.0 us)
Async XLA Ops:
  0.6 3.4 %copy-start = (bf16[4,8,4096]{2,1,0:T(8,128)(2,1)S(1)}, bf16[4,8,4096]{2,1,0:T(8,128)(2,1)}, u32[]{:S(2)}) copy-start(bf16[4,8,4096]{2,1,0:T(8,128)(2,1)} %param.19) | copy-start | bytes 786436
  0.6 5.4 %collective-permute-start = (s32[1,32]{1,0:T(1,128)}, s32[1,32]{1,0:T(1,128)S(1)}, u32[]{:S(2)}, u32[]{:S(2)}) collective-permute-start(s32[1,32]{1,0:T(1,128)} %atoms_ref.1), channel_id=1, source_target_pairs={{0,4},{4,0},{1,5},{5,1},{2,6},{6,2},{3,7},{7,3},{8,12},{12,8},{9,1... | collective-permute-start | bytes 392 | tf_op jit(solution)/shard_map/ppermute | solution.py:755
